TPU v7x, 128 devices: a whole 4x4x4 slice. The times are simulated.
128 devices in a mesh: dp: 32 (over y, x, core), tensor: 4 (over z).
Axes of the slice: x: 4, y: 4, z: 4, core: 2. Of those that a mesh axis runs over, the one named last changes fastest.
Arguments:
- acts: bfloat16 [2, 16384, 5120], P(None, 'dp', 'tensor'), may hold values from -6 to 6
- cotangent: bfloat16 [2, 16384, 5120], P(None, 'dp'), may hold values from -6 to 6
- q_start: float32 [2, 5120, 32], replicated, may hold values from -0.078125 to 0.078125
Outputs:
- p_factor: float32 [2, 5120, 32], P(None, 'tensor')
- q_factor: float32 [2, 5120, 32], replicated
All inputs are finite; a program needn't handle non-finite values.
Results may differ from a plain program's by a relative error of at most 0.0003.
Values sent between devices are 32-bit elements; how exact they have to be, the bound alone decides.
A program may use at most 192 MiB of HBM per device.

v0:
```python
import jax
import jax.numpy as jnp
from jax import lax
from jax.sharding import PartitionSpec as P


def orthonormal(p_rows, gram):
    lower = jnp.linalg.cholesky(gram)
    solved = jax.scipy.linalg.solve_triangular(lower, jnp.swapaxes(p_rows, 1, 2), lower=True)
    return jnp.swapaxes(solved, 1, 2)


def compress_layers(acts, cotangent, q_start, width):
    grads = jnp.einsum(
        "ltd,lte->lde", acts, cotangent, preferred_element_type=jnp.float32
    ) / lax.axis_size("dp")
    p_part = jnp.einsum("lde,ler->ldr", grads, q_start, precision=lax.Precision.HIGHEST)
    p_full = lax.psum(p_part, "dp")
    gram_part = jnp.einsum("ldr,lds->lrs", p_full, p_full, precision=lax.Precision.HIGHEST)
    gram = lax.psum(gram_part, "tensor")
    p_hat = orthonormal(p_full, gram)
    q_part = jnp.einsum("lde,ldr->ler", grads, p_hat, precision=lax.Precision.HIGHEST)
    q_new = lax.psum(q_part, ("dp", "tensor"))
    return (p_hat * jnp.sqrt(jnp.float32(width)), q_new)


def local(acts, cotangent, q_start):
    width = cotangent.shape[2]
    p_list = []
    q_list = []
    for layer in range(acts.shape[0]):
        p_one, q_one = compress_layers(
            acts[layer : layer + 1], cotangent[layer : layer + 1], q_start[layer : layer + 1], width
        )
        p_list.append(p_one)
        q_list.append(q_one)
    return (jnp.concatenate(p_list, 0), jnp.concatenate(q_list, 0))


def solution(mesh):
    placed = (P(None, "dp", "tensor"), P(None, "dp", None), P())
    return jax.shard_map(
        local, mesh=mesh, in_specs=placed, out_specs=(P(None, "tensor", None), P()), check_vma=False
    )
```

profile of v0, /device:TPU:1, one launch (start us, length us, event | category | flops | bytes accessed | tf_op | source)
XLA Modules:
  0.0 425.0 jit_solution(13452016796849240083)
XLA Ops:
  7.2 0.0 copy-start.3
  7.2 0.0 all-reduce.8.cloned.1.call-start
  7.2 0.0 copy-start.2
  7.2 15.1 %fusion.18 = f32[1280,5120]{1,0:T(8,128)} fusion(bf16[2,512,5120]{2,1,0:T(8,128)(2,1)} %param.7, bf16[2,512,1280]{2,1,0:T(8,128)(2,1)} %param.6), kind=kOutput, calls=%fused_computation.14 | convolution fusion | flops 6710886400 | bytes 32768000 | tf_op jit(solution)/shard_map/ltd,lte->lde/dot_general | solution.py:14
  22.3 0.0 copy-done.3
  22.3 0.0 copy-done.2
  22.3 0.0 copy-start
  22.3 12.4 %fusion.20 = f32[1280,5120]{1,0:T(8,128)} fusion(bf16[2,512,5120]{2,1,0:T(8,128)(2,1)S(1)} %copy-done.2, bf16[2,512,1280]{2,1,0:T(8,128)(2,1)S(1)} %copy-done.3), kind=kOutput, calls=%fused_computation.16 | convolution fusion | flops 6710886400 | bytes 32768000 | tf_op jit(solution)/shard_map/ltd,lte->lde/dot_general | solution.py:14
  34.7 0.0 copy-done
  34.7 28.0 %fusion.27 = f32[1,1280,32]{1,2,0:T(8,128)} fusion(f32[1280,5120]{1,0:T(8,128)} %fusion.18, f32[2,5120,32]{1,2,0:T(8,128)S(1)} %copy-done), kind=kOutput, calls=%fused_computation.21 | convolution fusion | flops 2523136000 | bytes 27033600 | tf_op jit(solution)/shard_map/lde,ler->ldr/dot_general | solution.py:17
  62.7 28.0 %fusion.24 = f32[1,1280,32]{1,2,0:T(8,128)} fusion(f32[1280,5120]{1,0:T(8,128)} %fusion.20, f32[2,5120,32]{1,2,0:T(8,128)S(1)} %copy-done), kind=kOutput, calls=%fused_computation.20 | convolution fusion | flops 2523136000 | bytes 27033600 | tf_op jit(solution)/shard_map/lde,ler->ldr/dot_general | solution.py:17
  90.7 0.0 all-reduce.8.cloned.1.call-update
  90.7 0.0 all-reduce.6.cloned.1.call-start
  90.7 105.0 %all-reduce.8.cloned.1.call-done = (f32[1,1280,32]{1,2,0:T(8,128)}, f32[1,1280,32]{1,2,0:T(8,128)}) async-done(((f32[1,1280,32]{1,2,0:T(8,128)}, f32[1,1280,32]{1,2,0:T(8,128)}), (f32[1,1280,32]{1,2,0:T(8,128)}, f32[1,1280,32]{1,2,0:T(8,128)})) %all-reduce.8.cloned.1.call-update) | async-done | bytes 327696 | tf_op jit(solution)/shard_map/psum | solution.py:18
  195.8 1.3 convolution_bitcast_fusion
  197.0 1.3 convolution_bitcast_fusion.1
  198.3 13.5 %all-reduce.2 = (f32[1,32,32]{1,2,0:T(8,128)S(1)}, f32[1,32,32]{1,2,0:T(8,128)S(1)}) all-reduce(f32[1,32,32]{1,2,0:T(8,128)S(1)} %convolution_bitcast_fusion, f32[1,32,32]{1,2,0:T(8,128)S(1)} %convolution_bitcast_fusion.1), channel_id=1, replica_groups=mesh['dp'=32,'tensor'=4] {'tensor'}, use_global_device_ids=true, to_apply=%region_5.0 | all-reduce | flops 2048 | bytes 16384 | tf_op jit(solution)/shard_map/psum | solution.py:20
  211.8 0.1 copy.8
  211.9 0.1 copy.6
  212.0 2.9 custom-call.10
  215.0 0.6 compare_reduce_fusion
  215.6 0.7 select_select_fusion
  216.3 2.4 custom-call.11
  218.7 1.3 fusion.38
  220.0 0.0 copy-start.1
  220.0 19.9 %fusion.15 = f32[1,5120,32]{1,2,0:T(8,128)} fusion(f32[32,1280]{1,0:T(8,128)S(1)} %fusion.38, f32[1280,5120]{1,0:T(8,128)} %fusion.18), kind=kOutput, calls=%fused_computation.13 | convolution fusion | flops 2523136000 | bytes 27033600 | tf_op jit(solution)/shard_map/lde,ldr->ler/dot_general | solution.py:22
  239.9 2.9 custom-call.8
  242.9 0.6 compare_reduce_fusion.1
  243.5 0.7 select_select_fusion.1
  244.2 2.4 custom-call.9
  246.6 0.0 copy-done.1
  246.6 0.4 fusion.40
  247.0 19.9 %fusion.12 = f32[1,5120,32]{1,2,0:T(8,128)} fusion(f32[32,1280]{1,0:T(8,128)S(1)} %fusion.40, f32[1280,5120]{1,0:T(8,128)} %fusion.20), kind=kOutput, calls=%fused_computation.12 | convolution fusion | flops 2523136000 | bytes 27033600 | tf_op jit(solution)/shard_map/lde,ldr->ler/dot_general | solution.py:22
  266.9 0.0 all-reduce.6.cloned.1.call-update
  266.9 0.8 pad_maximum_fusion.1
  267.7 148.0 %all-reduce.6.cloned.1.call-done = (f32[1,5120,32]{1,2,0:T(8,128)}, f32[1,5120,32]{1,2,0:T(8,128)}) async-done(((f32[1,5120,32]{1,2,0:T(8,128)}, f32[1,5120,32]{1,2,0:T(8,128)}), (f32[1,5120,32]{1,2,0:T(8,128)}, f32[1,5120,32]{1,2,0:T(8,128)})) %all-reduce.6.cloned.1.call-update) | async-done | bytes 1310736 | tf_op jit(solution)/shard_map/psum | solution.py:23
  415.7 2.4 pad_maximum_fusion
  (5 shorter events, 0.1 us)
Async XLA Ops:
  7.2 15.2 %copy-start.3 = (bf16[2,512,1280]{2,1,0:T(8,128)(2,1)S(1)}, bf16[2,512,1280]{2,1,0:T(8,128)(2,1)}, u32[]{:S(2)}) copy-start(bf16[2,512,1280]{2,1,0:T(8,128)(2,1)} %param.6) | copy-start | bytes 7864324
  7.2 188.6 %all-reduce.8.cloned.1.call-start = ((), (), s32[]{:S(2)}) async-start(), calls=%async_computation.1 | async-start | bytes 655360 | tf_op jit(solution)/shard_map/psum | solution.py:18
  7.2 15.1 %copy-start.2 = (bf16[2,512,5120]{2,1,0:T(8,128)(2,1)S(1)}, bf16[2,512,5120]{2,1,0:T(8,128)(2,1)}, u32[]{:S(2)}) copy-start(bf16[2,512,5120]{2,1,0:T(8,128)(2,1)} %param.7) | copy-start | bytes 31457284
  22.3 12.4 %copy-start = (f32[2,5120,32]{1,2,0:T(8,128)S(1)}, f32[2,5120,32]{1,2,0:T(8,128)}, u32[]{:S(2)}) copy-start(f32[2,5120,32]{1,2,0:T(8,128)} %param.8) | copy-start | bytes 3932164
  90.7 325.0 %all-reduce.6.cloned.1.call-start = ((), (), s32[]{:S(2)}) async-start(), calls=%async_computation | async-start | bytes 2621440 | tf_op jit(solution)/shard_map/psum | solution.py:23
  220.0 26.6 %copy-start.1 = (f32[1,1280,32]{1,2,0:T(8,128)S(1)}, f32[1,1280,32]{1,2,0:T(8,128)}, u32[]{:S(2)}) copy-start(f32[1,1280,32]{1,2,0:T(8,128)} %get-tuple-element.7) | copy-start | bytes 491524
Sparse Core Ops, SparseCore 0:
  90.8 104.9 all-reduce.7
  267.0 148.6 all-reduce.5
where the time goes:
time: 425 us
  waiting for transfers between devices  253 us (60%)
  matrix products  127 us (30%)
  other arithmetic  16.6 us (4%)
  between operations  14.2 us (3%)
  blocking collectives  13.5 us (3%)
    psum x1, waiting for transfers between devices, compress_layers(): q_new = lax.psum(q_part, ('dp', 'tensor'))  148 us
    psum x1, waiting for transfers between devices, compress_layers(): p_full = lax.psum(p_part, 'dp')  105 us
    dot_general x2, matrix products, compress_layers(): jnp.einsum('lde,ler->ldr', grads, q_start, precision=lax.Precision.HIGHEST)  56 us
    dot_general x2, matrix products, compress_layers(): jnp.einsum('lde,ldr->ler', grads, p_hat, precision=lax.Precision.HIGHEST)  39.8 us
    dot_general x2, matrix products, compress_layers(): jnp.einsum('ltd,lte->lde', acts, cotangent, preferred_element_type=jnp.fl...  27.5 us
    psum x1, blocking collectives, compress_layers(): gram = lax.psum(gram_part, 'tensor')  13.5 us
  transfers between devices with their start and end apart: 2, of which 2 were waited for; matrix products, arithmetic and copies ran while one was open for 0% of the time, Pallas kernels for 0%

commit v1 on v0

v1 whole, which is shorter than its diff:
```python
import functools

import jax
import jax.numpy as jnp
from jax import lax
from jax.experimental import pallas as pl
from jax.experimental.pallas import tpu as pltpu
from jax.sharding import PartitionSpec as P

MESH = pl.DeviceIdType.MESH
F32 = jnp.float32
BF16 = jnp.bfloat16
NN = (((1,), (0,)), ((), ()))
NT = (((1,), (1,)), ((), ()))
TILE = 128
FLY = 4


def dot(a, b, dims):
    return lax.dot_general(a, b, dims, preferred_element_type=F32)


def split3(x):
    hi = x.astype(BF16)
    rest = x - hi.astype(F32)
    mid = rest.astype(BF16)
    low = (rest - mid.astype(F32)).astype(BF16)
    return jnp.concatenate([hi, mid, low], axis=0)


def sum3(x):
    return x[0:32] + x[32:64] + x[64:96]


def to_pieces(ref, value):
    for j in range(16):
        g, h = j // 2, j % 2
        ref[j] = value[4 * g : 4 * g + 4, 640 * h : 640 * h + 640]


def from_pieces(ref):
    halves = []
    for h in range(2):
        halves.append(jnp.concatenate([ref[2 * g + h] for g in range(8)], axis=0))
    return jnp.concatenate(halves, axis=1)


def invert_factor(grams):
    rows = lax.broadcasted_iota(jnp.int32, (32, 128), 0)
    lanes = lax.broadcasted_iota(jnp.int32, (32, 128), 1)
    eye = jnp.where(rows == lanes % 32, 1.0, 0.0).astype(F32)
    work = jnp.where((lanes // 32) % 2 == 1, eye, grams)
    first = lanes < 64
    for k in range(32):
        row = work[k : k + 1, :]
        pivot = jnp.where(first[0:1], row[:, k : k + 1], row[:, 64 + k : 65 + k])
        scale = lax.rsqrt(pivot)
        scale = scale * (1.5 - 0.5 * pivot * scale * scale)
        column = jnp.where(first, work[:, k : k + 1], work[:, 64 + k : 65 + k])
        row = row * scale
        work = jnp.where(rows > k, work - (column * scale) * row, jnp.where(rows == k, row, work))
    return work


def exchange_kernel(
    a_hbm, c_hbm, q_hbm,
    zag, pag, inv_ref,
    a, c, q, q3t, wt, yt, px, pxr, ps, prr, zx, zxr, zs, zrr, gram,
    load_sem, core_sem, corer_sem, send_sem, prs_sem, pag_sem, pfw_sem, g_sem, zrs_sem, zag_sem, zfw_sem,
):
    dp = lax.axis_index("dp")
    z = lax.axis_index("tensor")
    core = lax.rem(dp, 2)
    plane = dp // 2
    y, x = plane // 4, lax.rem(plane, 4)
    mine, other = core, 1 - core
    sibling = {"dp": plane * 2 + other, "tensor": z}

    def peer(i):
        dz, dy, dx = i // 16, lax.rem(i // 4, 4), lax.rem(i, 4)
        to_plane = lax.rem(y + dy, 4) * 4 + lax.rem(x + dx, 4)
        to_z = lax.rem(z + dz, 4)
        return to_plane, to_z, {"dp": to_plane * 2 + core, "tensor": to_z}

    def source(i):
        dz, dy, dx = i // 16, lax.rem(i // 4, 4), lax.rem(i, 4)
        return lax.rem(y + 4 - dy, 4) * 4 + lax.rem(x + 4 - dx, 4), lax.rem(z + 4 - dz, 4)

    def remote(src, dst, send, recv, device):
        return pltpu.make_async_remote_copy(
            src_ref=src, dst_ref=dst, send_sem=send, recv_sem=recv, device_id=device, device_id_type=MESH
        )

    items = []
    for layer in (other, mine):
        items.append((q_hbm.at[layer], q.at[layer]))
    for layer in (other, mine):
        items.append((a_hbm.at[layer], a.at[layer]))
        for t in range(512 // TILE):
            items.append((c_hbm.at[layer, pl.ds(t * TILE, TILE)], c.at[layer, pl.ds(t * TILE, TILE)]))
    loads = [pltpu.make_async_copy(s, d, load_sem.at[i]) for i, (s, d) in enumerate(items)]
    for load in loads[:FLY]:
        load.start()

    barrier = pltpu.get_barrier_semaphore()

    def greet(i, carry):
        pl.semaphore_signal(barrier, inc=1, device_id=peer(i)[2], device_id_type=MESH)
        return carry

    pl.semaphore_signal(barrier, inc=1, device_id=sibling, device_id_type=MESH)
    lax.fori_loop(1, 64, greet, 0)

    def arrive(i):
        loads[i].wait()
        if i + FLY < len(loads):
            loads[i + FLY].start()

    for i, layer in enumerate((other, mine)):
        arrive(i)
        q3t[layer] = split3(q[layer]).T
    core_copies = []
    for n, layer in enumerate((other, mine)):
        base = 2 + n * (1 + 512 // TILE)
        arrive(base)
        for t in range(512 // TILE):
            arrive(base + 1 + t)
            w = dot(c[layer, t * TILE : (t + 1) * TILE, :], q3t[layer], NN)
            wt[:, t * TILE : (t + 1) * TILE] = sum3(w.T) * (1.0 / 32.0)
        part = sum3(dot(split3(wt[...]), a[layer], NN))
        if n == 0:
            to_pieces(px, part)
            pl.semaphore_wait(barrier, 64)
            core_copies.append(remote(px, pxr, core_sem.at[0], corer_sem.at[0], sibling))
            core_copies[0].start()
        else:
            to_pieces(ps, part)
    core_copies[0].wait_recv()
    ps[...] += pxr[...]

    sends = []
    for i in range(1, 16):
        to_plane, _, device = peer(i)
        cp = remote(ps.at[to_plane], prr.at[plane], send_sem.at[i], prs_sem.at[plane], device)
        cp.start()
        sends.append(cp)
    prr[plane] = ps[plane]
    for i in range(1, 16):
        from_plane, _ = source(i)
        remote(ps.at[0], prr.at[from_plane], send_sem.at[i], prs_sem.at[from_plane], sibling).wait_recv()
    pag[mine, plane] = jnp.sum(prr[...], axis=0)
    for cp in sends:
        cp.wait_send()

    sends = []
    for i in range(1, 16):
        _, _, device = peer(i)
        cp = remote(pag.at[mine, plane], pag.at[mine, plane], send_sem.at[i], pag_sem.at[plane], device)
        cp.start()
        sends.append(cp)
    cp = remote(pag.at[mine, plane], pag.at[mine, plane], send_sem.at[0], pfw_sem.at[plane], sibling)
    cp.start()
    sends.append(cp)
    forwards = []
    for i in range(1, 16):
        from_plane, _ = source(i)
        slot = pag.at[mine, from_plane]
        remote(slot, slot, send_sem.at[i], pag_sem.at[from_plane], sibling).wait_recv()
        cp = remote(slot, slot, send_sem.at[15 + i], pfw_sem.at[from_plane], sibling)
        cp.start()
        forwards.append(cp)

    def back(layer):
        p3 = split3(from_pieces(pag.at[layer]))
        yt[layer] = sum3(dot(p3, a[layer], NT)) * (1.0 / 32.0)
        g9 = dot(p3, p3, NT)
        g3 = sum3(g9)
        return g3[:, 0:32] + g3[:, 32:64] + g3[:, 64:96]

    g_mine = back(mine)
    for i in range(16):
        from_plane, _ = source(i)
        slot = pag.at[other, from_plane]
        remote(slot, slot, send_sem.at[i], pfw_sem.at[from_plane], sibling).wait_recv()
    g_other = back(other)
    for cp in sends + forwards:
        cp.wait_send()

    def z_part(layer, ref):
        y3 = split3(yt[layer])
        for b in range(4):
            to_pieces(ref.at[b], sum3(dot(y3, c[layer, :, b * 1280 : (b + 1) * 1280], NN)))

    z_part(other, zx)
    z_copy = remote(zx, zxr, core_sem.at[1], corer_sem.at[1], sibling)
    z_copy.start()
    zero = jnp.zeros((32, 32), F32)
    g_first = jnp.where(core == 0, g_mine, g_other)
    g_second = jnp.where(core == 0, g_other, g_mine)
    gram[z] = jnp.concatenate([g_first, zero, g_second, zero], axis=1)
    g_copies = []
    for dz in range(1, 4):
        device = {"dp": dp, "tensor": lax.rem(z + dz, 4)}
        cp = remote(gram.at[z], gram.at[z], send_sem.at[dz], g_sem.at[z], device)
        cp.start()
        g_copies.append(cp)
    z_part(mine, zs)
    z_copy.wait_recv()
    zs[...] += zxr[...]

    def scatter(i, carry):
        to_plane, to_z, device = peer(i)
        me = z * 16 + plane
        remote(zs.at[to_z, to_plane], zrr.at[me], send_sem.at[32 + i], zrs_sem.at[me], device).start()
        return carry

    lax.fori_loop(1, 64, scatter, 0)
    me = z * 16 + plane
    zrr[me] = zs[z, plane]
    for dz in range(1, 4):
        from_z = lax.rem(z + 4 - dz, 4)
        remote(gram.at[from_z], gram.at[from_z], send_sem.at[0], g_sem.at[from_z], sibling).wait_recv()
    inv_ref[...] = invert_factor(gram[0] + gram[1] + gram[2] + gram[3])

    def scattered(i, carry):
        from_plane, from_z = source(i)
        slot = from_z * 16 + from_plane
        remote(zrr.at[slot], zrr.at[slot], send_sem.at[0], zrs_sem.at[slot], sibling).wait_recv()
        return carry

    lax.fori_loop(1, 64, scattered, 0)
    zag[mine, me] = jnp.sum(zrr[...], axis=0)

    def scatter_done(i, carry):
        remote(zs.at[0, 0], zrr.at[0], send_sem.at[32 + i], zrs_sem.at[0], sibling).wait_send()
        return carry

    lax.fori_loop(1, 64, scatter_done, 0)

    own = zag.at[mine, me]

    def gather(i, carry):
        remote(own, own, send_sem.at[32 + i], zag_sem.at[me], peer(i)[2]).start()
        return carry

    lax.fori_loop(1, 64, gather, 0)
    remote(own, own, send_sem.at[32], zfw_sem.at[me], sibling).start()

    def forward(i, carry):
        from_plane, from_z = source(i)
        place = from_z * 16 + from_plane
        slot = zag.at[mine, place]
        remote(slot, slot, send_sem.at[0], zag_sem.at[place], sibling).wait_recv()
        remote(slot, slot, send_sem.at[96 + i], zfw_sem.at[place], sibling).start()
        return carry

    lax.fori_loop(1, 64, forward, 0)

    def forwarded(i, carry):
        from_plane, from_z = source(i)
        place = from_z * 16 + from_plane
        slot = zag.at[other, place]
        remote(slot, slot, send_sem.at[0], zfw_sem.at[place], sibling).wait_recv()
        return carry

    lax.fori_loop(0, 64, forwarded, 0)

    def sent(i, carry):
        remote(own, own, send_sem.at[32 + i], zag_sem.at[me], sibling).wait_send()
        return carry

    lax.fori_loop(0, 64, sent, 0)

    def forward_sent(i, carry):
        remote(own, own, send_sem.at[96 + i], zag_sem.at[me], sibling).wait_send()
        return carry

    lax.fori_loop(1, 64, forward_sent, 0)
    core_copies[0].wait_send()
    z_copy.wait_send()
    for cp in g_copies:
        cp.wait_send()


def finish_kernel(zag, pag, inv_ref, p_out, q_out, *, root):
    for layer in range(2):
        inverse = inv_ref[:, 64 * layer + 32 : 64 * layer + 64]
        pieces = split3(inverse)
        left = jnp.concatenate([pieces, pieces, pieces], axis=1)
        p_out[layer] = sum3(dot(left, split3(from_pieces(pag.at[layer])), NN)) * root
        for b in range(4):
            block = from_pieces(zag.at[layer, 16 * b : 16 * b + 16])
            q_out[layer, :, b * 1280 : (b + 1) * 1280] = sum3(dot(left, split3(block), NN))


def local(acts, cotangent, q_start):
    width = cotangent.shape[2]
    q_t = jnp.swapaxes(q_start, 1, 2)
    hbm = pl.BlockSpec(memory_space=pl.ANY)
    vmem = pl.BlockSpec(memory_space=pltpu.VMEM)
    dma = pltpu.SemaphoreType.DMA
    zag, pag, inverse = pl.pallas_call(
        exchange_kernel,
        out_shape=(
            jax.ShapeDtypeStruct((2, 64, 4, 640), F32),
            jax.ShapeDtypeStruct((2, 16, 4, 640), F32),
            jax.ShapeDtypeStruct((32, 128), F32),
        ),
        in_specs=[hbm] * 3,
        out_specs=(vmem, vmem, vmem),
        scratch_shapes=[
            pltpu.VMEM((2, 512, 1280), BF16),
            pltpu.VMEM((2, 512, 5120), BF16),
            pltpu.VMEM((2, 32, 5120), F32),
            pltpu.VMEM((2, 5120, 96), BF16),
            pltpu.VMEM((32, 512), F32),
            pltpu.VMEM((2, 32, 512), F32),
            pltpu.VMEM((16, 4, 640), F32),
            pltpu.VMEM((16, 4, 640), F32),
            pltpu.VMEM((16, 4, 640), F32),
            pltpu.VMEM((16, 4, 640), F32),
            pltpu.VMEM((4, 16, 4, 640), F32),
            pltpu.VMEM((4, 16, 4, 640), F32),
            pltpu.VMEM((4, 16, 4, 640), F32),
            pltpu.VMEM((64, 4, 640), F32),
            pltpu.VMEM((4, 32, 128), F32),
            dma((16,)), dma((2,)), dma((2,)), dma((160,)), dma((16,)), dma((16,)), dma((16,)),
            dma((4,)), dma((64,)), dma((64,)), dma((64,)),
        ],
        name="exchange",
        compiler_params=pltpu.CompilerParams(
            collective_id=0, has_side_effects=True, vmem_limit_bytes=50 * 2**20
        ),
    )(acts, cotangent, q_t)
    p_t, q_new = pl.pallas_call(
        functools.partial(finish_kernel, root=float(width) ** 0.5),
        out_shape=(
            jax.ShapeDtypeStruct((2, 32, 1280), F32),
            jax.ShapeDtypeStruct((2, 32, 5120), F32),
        ),
        in_specs=[vmem] * 3,
        out_specs=(vmem, vmem),
        name="finish",
        compiler_params=pltpu.CompilerParams(vmem_limit_bytes=32 * 2**20),
    )(zag, pag, inverse)
    return jnp.swapaxes(p_t, 1, 2), jnp.swapaxes(q_new, 1, 2)


def solution(mesh):
    placed = (P(None, "dp", "tensor"), P(None, "dp", None), P())
    return jax.shard_map(
        local, mesh=mesh, in_specs=placed, out_specs=(P(None, "tensor", None), P()), check_vma=False
    )
```

time: 425 us -> 62.9 us (0.15)
  waiting for transfers between devices: 253 us -> 0 us
  matrix products: 127 us -> 0 us
  Pallas kernels: 0 us -> 60.8 us
  other arithmetic: 16.6 us -> 0 us
  between operations: 14.2 us -> 0.65 us
  blocking collectives: 13.5 us -> 0 us
    psum x2 -> x0, waiting for transfers between devices: 253 us -> none  [the longest x1 148 us: compress_layers(): q_new = lax.psum(q_part, ('dp', 'tensor'))]
    dot_general x8 -> x0, matrix products: 126 us -> none  [the longest x2 56 us: compress_layers(): jnp.einsum('lde,ler->ldr', grads, q_start, precision=lax.Precision.HIGHEST)]
    pallas_call x0 -> x2, Pallas kernels: none -> 60.8 us  [the longest x1 58.9 us: local(): pl.pallas_call(exchange_kernel, out_shape=(jax.ShapeDtypeStruct((2, 64, 4...]
    psum x1 -> x0, blocking collectives: 13.5 us -> none  [compress_layers(): gram = lax.psum(gram_part, 'tensor')]
    another operation x10 -> x0, other arithmetic: 13.4 us -> none  [the longest x6 7.18 us: orthonormal(): lower = jnp.linalg.cholesky(gram)]
  transfers between devices with their start and end apart: 2 -> 0, of which waited for: 2 -> 0; matrix products, arithmetic and copies ran while one was open for 0% -> 0% of each run, Pallas kernels for 0% -> 0%
where the time goes in v1:
time: 62.9 us; the launch traced here: 62.8 us
  Pallas kernels  60.8 us (97%)
  local copies, waits for them, and re-layouts  1.31 us (2%)
  between operations  0.65 us (1%)
    pallas_call x1, Pallas kernels, local(): pl.pallas_call(exchange_kernel, out_shape=(jax.ShapeDtypeStruct((2, 64, 4...  58.9 us
    pallas_call x1, Pallas kernels, local(): pl.pallas_call(functools.partial(finish_kernel, root=float(width) ** 0.5)...  1.92 us
    unnamed x2, local copies, waits for them, and re-layouts  1.31 us

profile of v1, /device:TPU:1, one launch (start us, length us, event | category | flops | bytes accessed | tf_op | source)
XLA Modules:
  0.0 62.8 jit_solution(1023287433482573230)
XLA Ops:
  0.6 0.0 copy-start
  0.6 1.3 %copy-done = f32[2,5120,32]{1,2,0:T(8,128)S(1)} copy-done((f32[2,5120,32]{1,2,0:T(8,128)S(1)}, f32[2,5120,32]{1,2,0:T(8,128)}, u32[]{:S(2)}) %copy-start) | copy-done | bytes 1310744
  1.9 58.9 %exchange.1 = (f32[2,64,4,640]{3,2,1,0:T(4,128)S(1)}, f32[2,16,4,640]{3,2,1,0:T(4,128)S(1)}, f32[32,128]{1,0:T(8,128)S(1)}) custom-call(bf16[2,512,1280]{2,1,0:T(8,128)(2,1)} %a_hbm.1, bf16[2,512,5120]{2,1,0:T(8,128)(2,1)} %c_hbm.1, f32[2,32,5120]{2,1,0:T(8,128)S(1)} %bitcast.3), custom_call_target="tpu_custom_call" | custom-call | tf_op jit(solution)/shard_map/exchange/pallas_call | solution.py:302
  60.9 1.9 %finish.1 = (f32[2,32,1280]{2,1,0:T(8,128)}, f32[2,32,5120]{2,1,0:T(8,128)}) custom-call(f32[2,64,4,640]{3,2,1,0:T(4,128)S(1)} %get-tuple-element.7.zag, f32[2,16,4,640]{3,2,1,0:T(4,128)S(1)} %get-tuple-element.8.pag, f32[32,128]{1,0:T(8,128)S(1)} %get-tuple-element.9.inv_ref), custom_call_target="tpu_custom_call" | custom-call | tf_op jit(solution)/shard_map/finish/pallas_call | solution.py:335
Async XLA Ops:
  0.6 1.3 %copy-start = (f32[2,5120,32]{1,2,0:T(8,128)S(1)}, f32[2,5120,32]{1,2,0:T(8,128)}, u32[]{:S(2)}) copy-start(f32[2,5120,32]{1,2,0:T(8,128)} %param.5) | copy-start | bytes 3932164

commit v2 on v1

v2 whole, which is shorter than its diff:
```python
import functools

import jax
import jax.numpy as jnp
from jax import lax
from jax.experimental import pallas as pl
from jax.experimental.pallas import tpu as pltpu
from jax.sharding import PartitionSpec as P

MESH = pl.DeviceIdType.MESH
F32 = jnp.float32
BF16 = jnp.bfloat16
NN = (((1,), (0,)), ((), ()))
NT = (((1,), (1,)), ((), ()))
TILE = 128


def hops(offset):
    return sum(min(d, 4 - d) for d in offset)


OFFSETS = [(dz, dy, dx) for dz in range(4) for dy in range(4) for dx in range(4)]
CUBE = sorted([o for o in OFFSETS if hops(o) > 0], key=hops, reverse=True)
PLANE = [o for o in CUBE if o[0] == 0]
AXIS = [o for o in CUBE if o[1] == 0 and o[2] == 0]
FLY = 4


def dot(a, b, dims):
    return lax.dot_general(a, b, dims, preferred_element_type=F32)


def split3(x):
    hi = x.astype(BF16)
    rest = x - hi.astype(F32)
    mid = rest.astype(BF16)
    low = (rest - mid.astype(F32)).astype(BF16)
    return jnp.concatenate([hi, mid, low], axis=0)


def sum3(x):
    return x[0:32] + x[32:64] + x[64:96]


def to_pieces(ref, value):
    for j in range(16):
        g, h = j // 2, j % 2
        ref[j] = value[4 * g : 4 * g + 4, 640 * h : 640 * h + 640]


def from_pieces(ref):
    halves = []
    for h in range(2):
        halves.append(jnp.concatenate([ref[2 * g + h] for g in range(8)], axis=0))
    return jnp.concatenate(halves, axis=1)


def invert_factor(grams):
    rows = lax.broadcasted_iota(jnp.int32, (32, 128), 0)
    lanes = lax.broadcasted_iota(jnp.int32, (32, 128), 1)
    eye = jnp.where(rows == lanes % 32, 1.0, 0.0).astype(F32)
    work = jnp.where((lanes // 32) % 2 == 1, eye, grams)
    first = lanes < 64
    for k in range(32):
        row = work[k : k + 1, :]
        pivot = jnp.where(first[0:1], row[:, k : k + 1], row[:, 64 + k : 65 + k])
        scale = lax.rsqrt(pivot)
        scale = scale * (1.5 - 0.5 * pivot * scale * scale)
        column = jnp.where(first, work[:, k : k + 1], work[:, 64 + k : 65 + k])
        row = row * scale
        work = jnp.where(rows > k, work - (column * scale) * row, jnp.where(rows == k, row, work))
    return work


def exchange_kernel(
    a_hbm, c_hbm, q_hbm,
    zag, pag, inv_ref,
    a, c, q, q3t, wt, yt, px, pxr, ps, prr, zx, zxr, zs, zrr, gram,
    load_sem, core_sem, corer_sem, send_sem, prs_sem, pag_sem, pfw_sem, g_sem, zrs_sem, zag_sem, zfw_sem,
):
    dp = lax.axis_index("dp")
    z = lax.axis_index("tensor")
    core = lax.rem(dp, 2)
    plane = dp // 2
    y, x = plane // 4, lax.rem(plane, 4)
    mine, other = core, 1 - core
    sibling = {"dp": plane * 2 + other, "tensor": z}

    ys = [lax.rem(y + d, 4) for d in range(4)]
    xs = [lax.rem(x + d, 4) for d in range(4)]
    zs_at = [lax.rem(z + d, 4) for d in range(4)]

    def place(dz, dy, dx):
        return ys[dy] * 4 + xs[dx], zs_at[dz]

    def device(dz, dy, dx):
        to_plane, to_z = place(dz, dy, dx)
        return {"dp": to_plane * 2 + core, "tensor": to_z}

    def back_from(dz, dy, dx):
        return place((4 - dz) % 4, (4 - dy) % 4, (4 - dx) % 4)

    def remote(src, dst, send, recv, device):
        return pltpu.make_async_remote_copy(
            src_ref=src, dst_ref=dst, send_sem=send, recv_sem=recv, device_id=device, device_id_type=MESH
        )

    pending = []

    def drain():
        for done in pending:
            done()

    items = []
    for layer in (other, mine):
        items.append((q_hbm.at[layer], q.at[layer]))
    for layer in (other, mine):
        items.append((a_hbm.at[layer], a.at[layer]))
        for t in range(512 // TILE):
            items.append((c_hbm.at[layer, pl.ds(t * TILE, TILE)], c.at[layer, pl.ds(t * TILE, TILE)]))
    loads = [pltpu.make_async_copy(s, d, load_sem.at[i]) for i, (s, d) in enumerate(items)]
    for load in loads[:FLY]:
        load.start()

    barrier = pltpu.get_barrier_semaphore()

    pl.semaphore_signal(barrier, inc=1, device_id=sibling, device_id_type=MESH)
    for offset in PLANE + AXIS:
        pl.semaphore_signal(barrier, inc=1, device_id=device(*offset), device_id_type=MESH)

    def arrive(i):
        loads[i].wait()
        if i + FLY < len(loads):
            loads[i + FLY].start()

    for i, layer in enumerate((other, mine)):
        arrive(i)
        q3t[layer] = split3(q[layer]).T
    for n, layer in enumerate((other, mine)):
        base = 2 + n * (1 + 512 // TILE)
        arrive(base)
        for t in range(512 // TILE):
            arrive(base + 1 + t)
            w = dot(c[layer, t * TILE : (t + 1) * TILE, :], q3t[layer], NN)
            wt[:, t * TILE : (t + 1) * TILE] = sum3(w.T) * (1.0 / 32.0)
        part = sum3(dot(split3(wt[...]), a[layer], NN))
        if n == 0:
            to_pieces(px, part)
            pl.semaphore_wait(barrier, 1 + len(PLANE) + len(AXIS))
            p_copy = remote(px, pxr, core_sem.at[0], corer_sem.at[0], sibling)
            p_copy.start()
            pending.append(p_copy.wait_send)
        else:
            to_pieces(ps, part)
    p_copy.wait_recv()
    ps[...] += pxr[...]

    for offset in PLANE:
        to_plane, _ = place(*offset)
        remote(ps.at[to_plane], prr.at[plane], send_sem.at[0], prs_sem.at[0], device(*offset)).start()
    pending.append(remote(ps.at[pl.ds(0, 15)], prr.at[pl.ds(0, 15)], send_sem.at[0], prs_sem.at[0], sibling).wait_send)
    prr[plane] = ps[plane]
    remote(ps.at[pl.ds(0, 15)], prr.at[pl.ds(0, 15)], send_sem.at[0], prs_sem.at[0], sibling).wait_recv()
    pag[mine, plane] = jnp.sum(prr[...], axis=0)

    own = pag.at[mine, plane]
    many = pag.at[mine, pl.ds(0, 15)]
    for offset in PLANE:
        remote(own, own, send_sem.at[1], pag_sem.at[plane], device(*offset)).start()
    pending.append(remote(many, many, send_sem.at[1], pag_sem.at[0], sibling).wait_send)
    remote(own, own, send_sem.at[2], pfw_sem.at[0], sibling).start()
    for offset in reversed(PLANE):
        from_plane, _ = back_from(*offset)
        slot = pag.at[mine, from_plane]
        remote(slot, slot, send_sem.at[0], pag_sem.at[from_plane], sibling).wait_recv()
        remote(slot, slot, send_sem.at[2], pfw_sem.at[0], sibling).start()
    pending.append(remote(pag.at[mine], pag.at[mine], send_sem.at[2], pfw_sem.at[0], sibling).wait_send)

    def back(layer):
        p3 = split3(from_pieces(pag.at[layer]))
        yt[layer] = sum3(dot(p3, a[layer], NT)) * (1.0 / 32.0)
        g9 = dot(p3, p3, NT)
        g3 = sum3(g9)
        return g3[:, 0:32] + g3[:, 32:64] + g3[:, 64:96]

    g_mine = back(mine)
    remote(pag.at[other], pag.at[other], send_sem.at[2], pfw_sem.at[0], sibling).wait_recv()
    g_other = back(other)

    def z_part(y3, layer, b, ref):
        to_pieces(ref.at[b], sum3(dot(y3, c[layer, :, b * 1280 : (b + 1) * 1280], NN)))

    y3 = split3(yt[other])
    z_copies = []
    for b in range(4):
        z_part(y3, other, b, zx)
        cp = remote(zx.at[b], zxr.at[b], core_sem.at[1 + b], corer_sem.at[1 + b], sibling)
        cp.start()
        z_copies.append(cp)
        pending.append(cp.wait_send)
    zero = jnp.zeros((32, 32), F32)
    g_first = jnp.where(core == 0, g_mine, g_other)
    g_second = jnp.where(core == 0, g_other, g_mine)
    gram[z] = jnp.concatenate([g_first, zero, g_second, zero], axis=1)
    for offset in AXIS:
        remote(gram.at[z], gram.at[z], send_sem.at[3], g_sem.at[z], device(*offset)).start()
    pending.append(remote(gram.at[pl.ds(0, 3)], gram.at[pl.ds(0, 3)], send_sem.at[3], g_sem.at[0], sibling).wait_send)
    y3 = split3(yt[mine])
    for b in range(4):
        z_part(y3, mine, b, zs)
    for offset in AXIS:
        _, from_z = back_from(*offset)
        remote(gram.at[from_z], gram.at[from_z], send_sem.at[3], g_sem.at[from_z], sibling).wait_recv()
    for b in range(4):
        z_copies[b].wait_recv()
        zs[b] += zxr[b]

    me = z * 16 + plane
    for offset in CUBE:
        to_plane, to_z = place(*offset)
        remote(zs.at[to_z, to_plane], zrr.at[me], send_sem.at[4], zrs_sem.at[0], device(*offset)).start()
    most = zrr.at[pl.ds(0, 63)]
    pending.append(remote(most, most, send_sem.at[4], zrs_sem.at[0], sibling).wait_send)
    zrr[me] = zs[z, plane]
    inv_ref[...] = invert_factor(gram[0] + gram[1] + gram[2] + gram[3])
    remote(most, most, send_sem.at[4], zrs_sem.at[0], sibling).wait_recv()
    zag[mine, me] = jnp.sum(zrr[...], axis=0)

    own = zag.at[mine, me]
    for offset in CUBE:
        remote(own, own, send_sem.at[5], zag_sem.at[z], device(*offset)).start()
    for dz in (0, 1, 3, 2):
        _, from_z = back_from(dz, 0, 0)
        count = 15 if dz == 0 else 16
        block = zag.at[mine, pl.ds(from_z * 16, count)]
        remote(block, block, send_sem.at[6], zag_sem.at[from_z], sibling).wait_recv()
        block = zag.at[mine, pl.ds(from_z * 16, 16)]
        remote(block, block, send_sem.at[6], zfw_sem.at[0], sibling).start()
    remote(zag.at[other], zag.at[other], send_sem.at[6], zfw_sem.at[0], sibling).wait_recv()
    remote(zag.at[mine], zag.at[mine], send_sem.at[6], zfw_sem.at[0], sibling).wait_send()
    most = zag.at[mine, pl.ds(0, 63)]
    remote(most, most, send_sem.at[5], zag_sem.at[0], sibling).wait_send()
    drain()


def finish_kernel(zag, pag, inv_ref, p_out, q_out, *, root):
    for layer in range(2):
        inverse = inv_ref[:, 64 * layer + 32 : 64 * layer + 64]
        pieces = split3(inverse)
        left = jnp.concatenate([pieces, pieces, pieces], axis=1)
        p_out[layer] = sum3(dot(left, split3(from_pieces(pag.at[layer])), NN)) * root
        for b in range(4):
            block = from_pieces(zag.at[layer, 16 * b : 16 * b + 16])
            q_out[layer, :, b * 1280 : (b + 1) * 1280] = sum3(dot(left, split3(block), NN))


def local(acts, cotangent, q_start):
    width = cotangent.shape[2]
    q_t = jnp.swapaxes(q_start, 1, 2)
    hbm = pl.BlockSpec(memory_space=pltpu.HBM)
    vmem = pl.BlockSpec(memory_space=pltpu.VMEM)
    dma = pltpu.SemaphoreType.DMA
    zag, pag, inverse = pl.pallas_call(
        exchange_kernel,
        out_shape=(
            jax.ShapeDtypeStruct((2, 64, 4, 640), F32),
            jax.ShapeDtypeStruct((2, 16, 4, 640), F32),
            jax.ShapeDtypeStruct((32, 128), F32),
        ),
        in_specs=[hbm] * 3,
        out_specs=(vmem, vmem, vmem),
        scratch_shapes=[
            pltpu.VMEM((2, 512, 1280), BF16),
            pltpu.VMEM((2, 512, 5120), BF16),
            pltpu.VMEM((2, 32, 5120), F32),
            pltpu.VMEM((2, 5120, 96), BF16),
            pltpu.VMEM((32, 512), F32),
            pltpu.VMEM((2, 32, 512), F32),
            pltpu.VMEM((16, 4, 640), F32),
            pltpu.VMEM((16, 4, 640), F32),
            pltpu.VMEM((16, 4, 640), F32),
            pltpu.VMEM((16, 4, 640), F32),
            pltpu.VMEM((4, 16, 4, 640), F32),
            pltpu.VMEM((4, 16, 4, 640), F32),
            pltpu.VMEM((4, 16, 4, 640), F32),
            pltpu.VMEM((64, 4, 640), F32),
            pltpu.VMEM((4, 32, 128), F32),
            dma((16,)), dma((5,)), dma((5,)), dma((7,)), dma((1,)), dma((16,)), dma((1,)),
            dma((4,)), dma((1,)), dma((4,)), dma((1,)),
        ],
        name="exchange",
        compiler_params=pltpu.CompilerParams(
            collective_id=0, has_side_effects=True, vmem_limit_bytes=50 * 2**20
        ),
    )(acts, cotangent, q_t)
    p_t, q_new = pl.pallas_call(
        functools.partial(finish_kernel, root=float(width) ** 0.5),
        out_shape=(
            jax.ShapeDtypeStruct((2, 32, 1280), F32),
            jax.ShapeDtypeStruct((2, 32, 5120), F32),
        ),
        in_specs=[vmem] * 3,
        out_specs=(vmem, vmem),
        name="finish",
        compiler_params=pltpu.CompilerParams(vmem_limit_bytes=32 * 2**20),
    )(zag, pag, inverse)
    return jnp.swapaxes(p_t, 1, 2), jnp.swapaxes(q_new, 1, 2)


def solution(mesh):
    placed = (P(None, "dp", "tensor"), P(None, "dp", None), P())
    return jax.shard_map(
        local, mesh=mesh, in_specs=placed, out_specs=(P(None, "tensor", None), P()), check_vma=False
    )
```

time: 62.9 us -> 56 us (0.89)
  Pallas kernels: 60.8 us -> 53.9 us
    pallas_call x1, Pallas kernels: 58.9 us -> 52 us  [local(): pl.pallas_call(exchange_kernel, out_shape=(jax.ShapeDtypeStruct((2, 64, 4...]
where the time goes in v2:
time: 56 us; the launch traced here: 55.9 us
  Pallas kernels  53.9 us (96%)
  local copies, waits for them, and re-layouts  1.31 us (2%)
  between operations  0.65 us (1%)
    pallas_call x1, Pallas kernels, local(): pl.pallas_call(exchange_kernel, out_shape=(jax.ShapeDtypeStruct((2, 64, 4...  52 us
    pallas_call x1, Pallas kernels, local(): pl.pallas_call(functools.partial(finish_kernel, root=float(width) ** 0.5)...  1.92 us
    unnamed x2, local copies, waits for them, and re-layouts  1.31 us

profile of v2, /device:TPU:1, one launch (start us, length us, event | category | flops | bytes accessed | tf_op | source)
XLA Modules:
  0.0 55.9 jit_solution(5019037487232538528)
XLA Ops:
  0.6 0.0 copy-start
  0.6 1.3 %copy-done = f32[2,5120,32]{1,2,0:T(8,128)S(1)} copy-done((f32[2,5120,32]{1,2,0:T(8,128)S(1)}, f32[2,5120,32]{1,2,0:T(8,128)}, u32[]{:S(2)}) %copy-start) | copy-done | bytes 1310744
  1.9 52.0 %exchange.1 = (f32[2,64,4,640]{3,2,1,0:T(4,128)S(1)}, f32[2,16,4,640]{3,2,1,0:T(4,128)S(1)}, f32[32,128]{1,0:T(8,128)S(1)}) custom-call(bf16[2,512,1280]{2,1,0:T(8,128)(2,1)} %a_hbm.1, bf16[2,512,5120]{2,1,0:T(8,128)(2,1)} %c_hbm.1, f32[2,32,5120]{2,1,0:T(8,128)S(1)} %bitcast.3), custom_call_target="tpu_custom_call" | custom-call | tf_op jit(solution)/shard_map/exchange/pallas_call | solution.py:263
  53.9 1.9 %finish.1 = (f32[2,32,1280]{2,1,0:T(8,128)}, f32[2,32,5120]{2,1,0:T(8,128)}) custom-call(f32[2,64,4,640]{3,2,1,0:T(4,128)S(1)} %get-tuple-element.7.zag, f32[2,16,4,640]{3,2,1,0:T(4,128)S(1)} %get-tuple-element.8.pag, f32[32,128]{1,0:T(8,128)S(1)} %get-tuple-element.9.inv_ref), custom_call_target="tpu_custom_call" | custom-call | tf_op jit(solution)/shard_map/finish/pallas_call | solution.py:296
Async XLA Ops:
  0.6 1.3 %copy-start = (f32[2,5120,32]{1,2,0:T(8,128)S(1)}, f32[2,5120,32]{1,2,0:T(8,128)}, u32[]{:S(2)}) copy-start(f32[2,5120,32]{1,2,0:T(8,128)} %param.5) | copy-start | bytes 3932164

commit v3 on v2

--- a/solution.py
+++ b/solution.py
@@ -12,7 +12,7 @@
 BF16 = jnp.bfloat16
 NN = (((1,), (0,)), ((), ()))
 NT = (((1,), (1,)), ((), ()))
-TILE = 128
+TILE = 256
 
 
 def hops(offset):
@@ -23,7 +23,7 @@
 CUBE = sorted([o for o in OFFSETS if hops(o) > 0], key=hops, reverse=True)
 PLANE = [o for o in CUBE if o[0] == 0]
 AXIS = [o for o in CUBE if o[1] == 0 and o[2] == 0]
-FLY = 4
+FLY = 5
 
 
 def dot(a, b, dims):
@@ -76,7 +76,7 @@
     a_hbm, c_hbm, q_hbm,
     zag, pag, inv_ref,
     a, c, q, q3t, wt, yt, px, pxr, ps, prr, zx, zxr, zs, zrr, gram,
-    load_sem, core_sem, corer_sem, send_sem, prs_sem, pag_sem, pfw_sem, g_sem, zrs_sem, zag_sem, zfw_sem,
+    load_sem, core_sem, corer_sem, send_sem, prs_sem, pag_sem, pfw_sem, g_sem, zrs_sem, zag_sem, zfw_sem, near_sem,
 ):
     dp = lax.axis_index("dp")
     z = lax.axis_index("tensor")
@@ -161,6 +161,8 @@
     pending.append(remote(ps.at[pl.ds(0, 15)], prr.at[pl.ds(0, 15)], send_sem.at[0], prs_sem.at[0], sibling).wait_send)
     prr[plane] = ps[plane]
     remote(ps.at[pl.ds(0, 15)], prr.at[pl.ds(0, 15)], send_sem.at[0], prs_sem.at[0], sibling).wait_recv()
+    for offset in AXIS:
+        pl.semaphore_signal(near_sem, inc=1, device_id=device(*offset), device_id_type=MESH)
     pag[mine, plane] = jnp.sum(prr[...], axis=0)
 
     own = pag.at[mine, plane]
@@ -208,20 +210,21 @@
     y3 = split3(yt[mine])
     for b in range(4):
         z_part(y3, mine, b, zs)
-    for offset in AXIS:
-        _, from_z = back_from(*offset)
-        remote(gram.at[from_z], gram.at[from_z], send_sem.at[3], g_sem.at[from_z], sibling).wait_recv()
     for b in range(4):
         z_copies[b].wait_recv()
         zs[b] += zxr[b]
 
     me = z * 16 + plane
+    pl.semaphore_wait(near_sem, len(AXIS))
     for offset in CUBE:
         to_plane, to_z = place(*offset)
         remote(zs.at[to_z, to_plane], zrr.at[me], send_sem.at[4], zrs_sem.at[0], device(*offset)).start()
     most = zrr.at[pl.ds(0, 63)]
     pending.append(remote(most, most, send_sem.at[4], zrs_sem.at[0], sibling).wait_send)
     zrr[me] = zs[z, plane]
+    for offset in AXIS:
+        _, from_z = back_from(*offset)
+        remote(gram.at[from_z], gram.at[from_z], send_sem.at[3], g_sem.at[from_z], sibling).wait_recv()
     inv_ref[...] = invert_factor(gram[0] + gram[1] + gram[2] + gram[3])
     remote(most, most, send_sem.at[4], zrs_sem.at[0], sibling).wait_recv()
     zag[mine, me] = jnp.sum(zrr[...], axis=0)
@@ -286,11 +289,11 @@
             pltpu.VMEM((64, 4, 640), F32),
             pltpu.VMEM((4, 32, 128), F32),
             dma((16,)), dma((5,)), dma((5,)), dma((7,)), dma((1,)), dma((16,)), dma((1,)),
-            dma((4,)), dma((1,)), dma((4,)), dma((1,)),
+            dma((4,)), dma((1,)), dma((4,)), dma((1,)), pltpu.SemaphoreType.REGULAR,
         ],
         name="exchange",
         compiler_params=pltpu.CompilerParams(
-            collective_id=0, has_side_effects=True, vmem_limit_bytes=50 * 2**20
+            collective_id=0, has_side_effects=True, vmem_limit_bytes=52 * 2**20
         ),
     )(acts, cotangent, q_t)
     p_t, q_new = pl.pallas_call(

time: 56 us -> 51.9 us (0.927)
  Pallas kernels: 53.9 us -> 51.2 us
  local copies, waits for them, and re-layouts: 1.31 us -> 0 us
    pallas_call x1, Pallas kernels: 52 us -> 49.3 us  [local(): pl.pallas_call(exchange_kernel, out_shape=(jax.ShapeDtypeStruct((2, 64, 4...]
    unnamed x2 -> x0, local copies, waits for them, and re-layouts: 1.31 us -> none
where the time goes in v3:
time: 51.9 us; the launch traced here: 51.8 us
  Pallas kernels  51.2 us (99%)
  between operations  0.64 us (1%)
    pallas_call x1, Pallas kernels, local(): pl.pallas_call(exchange_kernel, out_shape=(jax.ShapeDtypeStruct((2, 64, 4...  49.3 us
    pallas_call x1, Pallas kernels, local(): pl.pallas_call(functools.partial(finish_kernel, root=float(width) ** 0.5)...  1.92 us

profile of v3, /device:TPU:1, one launch (start us, length us, event | category | flops | bytes accessed | tf_op | source)
XLA Modules:
  0.0 51.8 jit_solution(17621440856369984097)
XLA Ops:
  0.6 49.3 %exchange.1 = (f32[2,64,4,640]{3,2,1,0:T(4,128)S(1)}, f32[2,16,4,640]{3,2,1,0:T(4,128)S(1)}, f32[32,128]{1,0:T(8,128)S(1)}) custom-call(bf16[2,512,1280]{2,1,0:T(8,128)(2,1)} %a_hbm.1, bf16[2,512,5120]{2,1,0:T(8,128)(2,1)} %c_hbm.1, f32[2,32,5120]{2,1,0:T(8,128)} %bitcast.3), custom_call_target="tpu_custom_call" | custom-call | tf_op jit(solution)/shard_map/exchange/pallas_call | solution.py:266
  49.9 1.9 %finish.1 = (f32[2,32,1280]{2,1,0:T(8,128)}, f32[2,32,5120]{2,1,0:T(8,128)}) custom-call(f32[2,64,4,640]{3,2,1,0:T(4,128)S(1)} %get-tuple-element.7.zag, f32[2,16,4,640]{3,2,1,0:T(4,128)S(1)} %get-tuple-element.8.pag, f32[32,128]{1,0:T(8,128)S(1)} %get-tuple-element.9.inv_ref), custom_call_target="tpu_custom_call" | custom-call | tf_op jit(solution)/shard_map/finish/pallas_call | solution.py:299

commit v4 on v3

--- a/solution.py
+++ b/solution.py
@@ -13,6 +13,8 @@
 NN = (((1,), (0,)), ((), ()))
 NT = (((1,), (1,)), ((), ()))
 TILE = 256
+WIDTHS = (1792, 1792, 1536)
+STARTS = (0, 1792, 3584)
 
 
 def hops(offset):
@@ -43,9 +45,10 @@
 
 
 def to_pieces(ref, value):
+    half = value.shape[1] // 2
     for j in range(16):
         g, h = j // 2, j % 2
-        ref[j] = value[4 * g : 4 * g + 4, 640 * h : 640 * h + 640]
+        ref[j] = value[4 * g : 4 * g + 4, half * h : half * h + half]
 
 
 def from_pieces(ref):
@@ -74,9 +77,11 @@
 
 def exchange_kernel(
     a_hbm, c_hbm, q_hbm,
-    zag, pag, inv_ref,
-    a, c, q, q3t, wt, yt, px, pxr, ps, prr, zx, zxr, zs, zrr, gram,
-    load_sem, core_sem, corer_sem, send_sem, prs_sem, pag_sem, pfw_sem, g_sem, zrs_sem, zag_sem, zfw_sem, near_sem,
+    zag0, zag1, zag2, pag, inv_ref,
+    a, c, q, q3t, wt, yt, px, pxr, ps, prr, gram,
+    zx0, zx1, zx2, zxr0, zxr1, zxr2, zs0, zs1, zs2, zrr0, zrr1, zrr2, zl0, zl1, zl2,
+    load_sem, core_sem, corer_sem, send_sem, prs_sem, pag_sem, pfw_sem, g_sem,
+    zsend_sem, zrs_sem, zline_sem, zag_sem, zfw_sem, near_sem,
 ):
     dp = lax.axis_index("dp")
     z = lax.axis_index("tensor")
@@ -99,6 +104,20 @@
 
     def back_from(dz, dy, dx):
         return place((4 - dz) % 4, (4 - dy) % 4, (4 - dx) % 4)
+
+    zag, zx, zxr = (zag0, zag1, zag2), (zx0, zx1, zx2), (zxr0, zxr1, zxr2)
+    zs, zrr, zl = (zs0, zs1, zs2), (zrr0, zrr1, zrr2), (zl0, zl1, zl2)
+
+    def spin(k, du, dv, dw):
+        return ((dw, du, dv), (dv, dw, du), (du, dv, dw))[k]
+
+    def seat(k, offset):
+        dz, dy, dx = offset
+        u, v = ((ys[dy], xs[dx]), (xs[dx], zs_at[dz]), (zs_at[dz], ys[dy]))[k]
+        return u * 4 + v
+
+    def line_at(k):
+        return (z, y, x)[k]
 
     def remote(src, dst, send, recv, device):
         return pltpu.make_async_remote_copy(
@@ -189,14 +208,14 @@
     remote(pag.at[other], pag.at[other], send_sem.at[2], pfw_sem.at[0], sibling).wait_recv()
     g_other = back(other)
 
-    def z_part(y3, layer, b, ref):
-        to_pieces(ref.at[b], sum3(dot(y3, c[layer, :, b * 1280 : (b + 1) * 1280], NN)))
+    def z_part(y3, layer, k, ref):
+        to_pieces(ref, sum3(dot(y3, c[layer, :, STARTS[k] : STARTS[k] + WIDTHS[k]], NN)))
 
     y3 = split3(yt[other])
     z_copies = []
-    for b in range(4):
-        z_part(y3, other, b, zx)
-        cp = remote(zx.at[b], zxr.at[b], core_sem.at[1 + b], corer_sem.at[1 + b], sibling)
+    for k in range(3):
+        z_part(y3, other, k, zx[k])
+        cp = remote(zx[k], zxr[k], core_sem.at[1 + k], corer_sem.at[1 + k], sibling)
         cp.start()
         z_copies.append(cp)
         pending.append(cp.wait_send)
@@ -208,53 +227,67 @@
         remote(gram.at[z], gram.at[z], send_sem.at[3], g_sem.at[z], device(*offset)).start()
     pending.append(remote(gram.at[pl.ds(0, 3)], gram.at[pl.ds(0, 3)], send_sem.at[3], g_sem.at[0], sibling).wait_send)
     y3 = split3(yt[mine])
-    for b in range(4):
-        z_part(y3, mine, b, zs)
-    for b in range(4):
-        z_copies[b].wait_recv()
-        zs[b] += zxr[b]
-
-    me = z * 16 + plane
-    pl.semaphore_wait(near_sem, len(AXIS))
-    for offset in CUBE:
-        to_plane, to_z = place(*offset)
-        remote(zs.at[to_z, to_plane], zrr.at[me], send_sem.at[4], zrs_sem.at[0], device(*offset)).start()
-    most = zrr.at[pl.ds(0, 63)]
-    pending.append(remote(most, most, send_sem.at[4], zrs_sem.at[0], sibling).wait_send)
-    zrr[me] = zs[z, plane]
+
+    def all_of(ref, count, send, recv):
+        view = ref.at[pl.ds(0, count)]
+        return remote(view, view, send, recv, sibling)
+
+    for k in range(3):
+        z_part(y3, mine, k, zs[k])
+        z_copies[k].wait_recv()
+        zs[k][...] += zxr[k][...]
+        if k == 0:
+            pl.semaphore_wait(near_sem, len(AXIS))
+        me = seat(k, (0, 0, 0))
+        for _, du, dv in PLANE:
+            offset = spin(k, du, dv, 0)
+            remote(
+                zs[k].at[seat(k, offset)], zrr[k].at[me], zsend_sem.at[k, 0], zrs_sem.at[k], device(*offset)
+            ).start()
+        pending.append(all_of(zs[k], 15, zsend_sem.at[k, 0], zrs_sem.at[k]).wait_send)
+        zrr[k][me] = zs[k][me]
+
     for offset in AXIS:
         _, from_z = back_from(*offset)
         remote(gram.at[from_z], gram.at[from_z], send_sem.at[3], g_sem.at[from_z], sibling).wait_recv()
     inv_ref[...] = invert_factor(gram[0] + gram[1] + gram[2] + gram[3])
-    remote(most, most, send_sem.at[4], zrs_sem.at[0], sibling).wait_recv()
-    zag[mine, me] = jnp.sum(zrr[...], axis=0)
-
-    own = zag.at[mine, me]
-    for offset in CUBE:
-        remote(own, own, send_sem.at[5], zag_sem.at[z], device(*offset)).start()
-    for dz in (0, 1, 3, 2):
-        _, from_z = back_from(dz, 0, 0)
-        count = 15 if dz == 0 else 16
-        block = zag.at[mine, pl.ds(from_z * 16, count)]
-        remote(block, block, send_sem.at[6], zag_sem.at[from_z], sibling).wait_recv()
-        block = zag.at[mine, pl.ds(from_z * 16, 16)]
-        remote(block, block, send_sem.at[6], zfw_sem.at[0], sibling).start()
-    remote(zag.at[other], zag.at[other], send_sem.at[6], zfw_sem.at[0], sibling).wait_recv()
-    remote(zag.at[mine], zag.at[mine], send_sem.at[6], zfw_sem.at[0], sibling).wait_send()
-    most = zag.at[mine, pl.ds(0, 63)]
-    remote(most, most, send_sem.at[5], zag_sem.at[0], sibling).wait_send()
+
+    for k in range(3):
+        all_of(zrr[k], 15, zsend_sem.at[k, 0], zrs_sem.at[k]).wait_recv()
+        w = line_at(k)
+        zl[k][w] = jnp.sum(zrr[k][...], axis=0)
+        for dw, _, _ in AXIS:
+            remote(
+                zl[k].at[w], zl[k].at[w], zsend_sem.at[k, 1], zline_sem.at[k], device(*spin(k, 0, 0, dw))
+            ).start()
+        pending.append(all_of(zl[k], 3, zsend_sem.at[k, 1], zline_sem.at[k]).wait_send)
+    for k in range(3):
+        all_of(zl[k], 3, zsend_sem.at[k, 1], zline_sem.at[k]).wait_recv()
+        me = seat(k, (0, 0, 0))
+        zag[k][mine, me] = zl[k][0] + zl[k][1] + zl[k][2] + zl[k][3]
+        own = zag[k].at[mine, me]
+        for _, du, dv in PLANE:
+            remote(own, own, zsend_sem.at[k, 2], zag_sem.at[k], device(*spin(k, du, dv, 0))).start()
+        pending.append(all_of(zag[k].at[mine], 15, zsend_sem.at[k, 2], zag_sem.at[k]).wait_send)
+    for k in range(3):
+        all_of(zag[k].at[mine], 15, zsend_sem.at[k, 2], zag_sem.at[k]).wait_recv()
+        cp = remote(zag[k].at[mine], zag[k].at[mine], zsend_sem.at[k, 3], zfw_sem.at[k], sibling)
+        cp.start()
+        pending.append(cp.wait_send)
+    for k in range(3):
+        remote(zag[k].at[other], zag[k].at[other], zsend_sem.at[k, 3], zfw_sem.at[k], sibling).wait_recv()
     drain()
 
 
-def finish_kernel(zag, pag, inv_ref, p_out, q_out, *, root):
+def finish_kernel(zag0, zag1, zag2, pag, inv_ref, p_out, q_out, *, root):
     for layer in range(2):
         inverse = inv_ref[:, 64 * layer + 32 : 64 * layer + 64]
         pieces = split3(inverse)
         left = jnp.concatenate([pieces, pieces, pieces], axis=1)
         p_out[layer] = sum3(dot(left, split3(from_pieces(pag.at[layer])), NN)) * root
-        for b in range(4):
-            block = from_pieces(zag.at[layer, 16 * b : 16 * b + 16])
-            q_out[layer, :, b * 1280 : (b + 1) * 1280] = sum3(dot(left, split3(block), NN))
+        for zag, start, width in zip((zag0, zag1, zag2), STARTS, WIDTHS):
+            block = from_pieces(zag.at[layer])
+            q_out[layer, :, start : start + width] = sum3(dot(left, split3(block), NN))
 
 
 def local(acts, cotangent, q_start):
@@ -263,15 +296,15 @@
     hbm = pl.BlockSpec(memory_space=pltpu.HBM)
     vmem = pl.BlockSpec(memory_space=pltpu.VMEM)
     dma = pltpu.SemaphoreType.DMA
-    zag, pag, inverse = pl.pallas_call(
+    *gathered, inverse = pl.pallas_call(
         exchange_kernel,
         out_shape=(
-            jax.ShapeDtypeStruct((2, 64, 4, 640), F32),
+            *[jax.ShapeDtypeStruct((2, 16, 4, width // 2), F32) for width in WIDTHS],
             jax.ShapeDtypeStruct((2, 16, 4, 640), F32),
             jax.ShapeDtypeStruct((32, 128), F32),
         ),
         in_specs=[hbm] * 3,
-        out_specs=(vmem, vmem, vmem),
+        out_specs=(vmem,) * 5,
         scratch_shapes=[
             pltpu.VMEM((2, 512, 1280), BF16),
             pltpu.VMEM((2, 512, 5120), BF16),
@@ -283,13 +316,11 @@
             pltpu.VMEM((16, 4, 640), F32),
             pltpu.VMEM((16, 4, 640), F32),
             pltpu.VMEM((16, 4, 640), F32),
-            pltpu.VMEM((4, 16, 4, 640), F32),
-            pltpu.VMEM((4, 16, 4, 640), F32),
-            pltpu.VMEM((4, 16, 4, 640), F32),
-            pltpu.VMEM((64, 4, 640), F32),
             pltpu.VMEM((4, 32, 128), F32),
+            *[pltpu.VMEM((16, 4, width // 2), F32) for _ in range(4) for width in WIDTHS],
+            *[pltpu.VMEM((4, 4, width // 2), F32) for width in WIDTHS],
             dma((16,)), dma((5,)), dma((5,)), dma((7,)), dma((1,)), dma((16,)), dma((1,)),
-            dma((4,)), dma((1,)), dma((4,)), dma((1,)), pltpu.SemaphoreType.REGULAR,
+            dma((4,)), dma((3, 4)), dma((3,)), dma((3,)), dma((3,)), dma((3,)), pltpu.SemaphoreType.REGULAR,
         ],
         name="exchange",
         compiler_params=pltpu.CompilerParams(
@@ -302,11 +333,11 @@
             jax.ShapeDtypeStruct((2, 32, 1280), F32),
             jax.ShapeDtypeStruct((2, 32, 5120), F32),
         ),
-        in_specs=[vmem] * 3,
+        in_specs=[vmem] * 5,
         out_specs=(vmem, vmem),
         name="finish",
         compiler_params=pltpu.CompilerParams(vmem_limit_bytes=32 * 2**20),
-    )(zag, pag, inverse)
+    )(*gathered, inverse)
     return jnp.swapaxes(p_t, 1, 2), jnp.swapaxes(q_new, 1, 2)
 
 

time: 51.9 us -> 49 us (0.944)
  Pallas kernels: 51.2 us -> 48.2 us
    pallas_call x1, Pallas kernels: 49.3 us -> 46.3 us  [local(): pl.pallas_call(exchange_kernel, out_shape=(*[jax.ShapeDtypeStruct((2, 16,...]
where the time goes in v4:
time: 49 us; the launch traced here: 48.9 us
  Pallas kernels  48.2 us (98%)
  between operations  0.64 us (1%)
    pallas_call x1, Pallas kernels, local(): pl.pallas_call(exchange_kernel, out_shape=(*[jax.ShapeDtypeStruct((2, 16,...  46.3 us
    pallas_call x1, Pallas kernels, local(): pl.pallas_call(functools.partial(finish_kernel, root=float(width) ** 0.5)...  1.92 us

profile of v4, /device:TPU:1, one launch (start us, length us, event | category | flops | bytes accessed | tf_op | source)
XLA Modules:
  0.0 48.9 jit_solution(6307676954660824156)
XLA Ops:
  0.6 46.3 %exchange.1 = (f32[2,16,4,896]{3,2,1,0:T(4,128)S(1)}, f32[2,16,4,896]{3,2,1,0:T(4,128)S(1)}, f32[2,16,4,768]{3,2,1,0:T(4,128)S(1)}, f32[2,16,4,640]{3,2,1,0:T(4,128)S(1)}, f32[32,128]{1,0:T(8,128)S(1)}) custom-call(bf16[2,512,1280]{2,1,0:T(8,128)(2,1)} %a_hbm.1, bf16[2,512,5120]{2,1,0:T(8,128)(2,1)} %c_hbm.1, f32[2,32,5120]{2,1,0:T(8,128)} %bitcast.3), custom_call_target="tpu_custom_call" | custom-call | tf_op jit(solution)/shard_map/exchange/pallas_call | solution.py:299
  47.0 1.9 %finish.1 = (f32[2,32,1280]{2,1,0:T(8,128)}, f32[2,32,5120]{2,1,0:T(8,128)}) custom-call(f32[2,16,4,896]{3,2,1,0:T(4,128)S(1)} %get-tuple-element.9.zag0, f32[2,16,4,896]{3,2,1,0:T(4,128)S(1)} %get-tuple-element.10.zag1, f32[2,16,4,768]{3,2,1,0:T(4,128)S(1)} %get-tuple-element.11.zag2, f32[2,16,4,640]{3,2,1,0:T(4,128)S(1)} %get-tuple-element.12.pag, ...), custom_call_target="tpu_custom_call" | custom-call | tf_op jit(solution)/shard_map/finish/pallas_call | solution.py:330

commit v5 on v4

v5 whole, which is shorter than its diff:
```python
import functools

import jax
import jax.numpy as jnp
from jax import lax
from jax.experimental import pallas as pl
from jax.experimental.pallas import tpu as pltpu
from jax.sharding import PartitionSpec as P

MESH = pl.DeviceIdType.MESH
F32 = jnp.float32
BF16 = jnp.bfloat16
NN = (((1,), (0,)), ((), ()))
NT = (((1,), (1,)), ((), ()))
TILE = 256
WIDTHS = (2048, 1536, 1536)
STARTS = (0, 2048, 3584)
P_WIDTHS = (768, 512)
P_STARTS = (0, 768)


def hops(offset):
    return sum(min(d, 4 - d) for d in offset)


OFFSETS = [(dz, dy, dx) for dz in range(4) for dy in range(4) for dx in range(4)]
CUBE = sorted([o for o in OFFSETS if hops(o) > 0], key=hops, reverse=True)
PLANE = [o for o in CUBE if o[0] == 0]
AXIS = [o for o in CUBE if o[1] == 0 and o[2] == 0]
FLY = 5


def dot(a, b, dims):
    return lax.dot_general(a, b, dims, preferred_element_type=F32)


def split3(x):
    hi = x.astype(BF16)
    rest = x - hi.astype(F32)
    mid = rest.astype(BF16)
    low = (rest - mid.astype(F32)).astype(BF16)
    return jnp.concatenate([hi, mid, low], axis=0)


def sum3(x):
    return x[0:32] + x[32:64] + x[64:96]


def to_pieces(ref, value):
    quarter = value.shape[1] // 4
    for j in range(16):
        g, h = j // 4, j % 4
        ref[j] = value[8 * g : 8 * g + 8, quarter * h : quarter * h + quarter]


def from_pieces(ref):
    bands = []
    for g in range(4):
        bands.append(jnp.concatenate([ref[4 * g + h] for h in range(4)], axis=1))
    return jnp.concatenate(bands, axis=0)


def invert_factor(grams):
    rows = lax.broadcasted_iota(jnp.int32, (32, 128), 0)
    lanes = lax.broadcasted_iota(jnp.int32, (32, 128), 1)
    eye = jnp.where(rows == lanes % 32, 1.0, 0.0).astype(F32)
    work = jnp.where((lanes // 32) % 2 == 1, eye, grams)
    first = lanes < 64
    for k in range(32):
        row = work[k : k + 1, :]
        pivot = jnp.where(first[0:1], row[:, k : k + 1], row[:, 64 + k : 65 + k])
        scale = lax.rsqrt(pivot)
        scale = scale * (1.5 - 0.5 * pivot * scale * scale)
        column = jnp.where(first, work[:, k : k + 1], work[:, 64 + k : 65 + k])
        row = row * scale
        work = jnp.where(rows > k, work - (column * scale) * row, jnp.where(rows == k, row, work))
    return work


def exchange_kernel(
    a_hbm, c_hbm, q_hbm,
    zag0, zag1, zag2, pf0, pf1, inv_ref,
    a, c, q, q3t, wt, px0, px1, pxr0, pxr1, pa0, pa1, pb0, pb1, gram,
    zx0, zx1, zx2, zxr0, zxr1, zxr2, zs0, zs1, zs2, zrr0, zrr1, zrr2, zl0, zl1, zl2,
    load_sem, core_sem, corer_sem, psend_sem, pa_sem, pb_sem, pfw_sem, gsend_sem, g_sem,
    zsend_sem, zrs_sem, zline_sem, zag_sem, zfw_sem, near_sem,
):
    dp = lax.axis_index("dp")
    z = lax.axis_index("tensor")
    core = lax.rem(dp, 2)
    plane = dp // 2
    y, x = plane // 4, lax.rem(plane, 4)
    mine, other = core, 1 - core
    sibling = {"dp": plane * 2 + other, "tensor": z}

    ys = [lax.rem(y + d, 4) for d in range(4)]
    xs = [lax.rem(x + d, 4) for d in range(4)]
    zs_at = [lax.rem(z + d, 4) for d in range(4)]

    def place(dz, dy, dx):
        return ys[dy] * 4 + xs[dx], zs_at[dz]

    def device(dz, dy, dx):
        to_plane, to_z = place(dz, dy, dx)
        return {"dp": to_plane * 2 + core, "tensor": to_z}

    def back_from(dz, dy, dx):
        return place((4 - dz) % 4, (4 - dy) % 4, (4 - dx) % 4)

    px, pxr, pa, pb, pf = (px0, px1), (pxr0, pxr1), (pa0, pa1), (pb0, pb1), (pf0, pf1)
    zag, zx, zxr = (zag0, zag1, zag2), (zx0, zx1, zx2), (zxr0, zxr1, zxr2)
    zs, zrr, zl = (zs0, zs1, zs2), (zrr0, zrr1, zrr2), (zl0, zl1, zl2)

    first, second = jnp.where(core == 0, x, y), jnp.where(core == 0, y, x)

    def along_first(d):
        row, column = jnp.where(core == 0, y, ys[d]), jnp.where(core == 0, xs[d], x)
        return {"dp": (row * 4 + column) * 2 + core, "tensor": z}

    def along_second(d):
        row, column = jnp.where(core == 0, ys[d], y), jnp.where(core == 0, x, xs[d])
        return {"dp": (row * 4 + column) * 2 + core, "tensor": z}

    def spin(k, du, dv, dw):
        return ((dw, du, dv), (dv, dw, du), (du, dv, dw))[k]

    def seat(k, offset):
        dz, dy, dx = offset
        u, v = ((ys[dy], xs[dx]), (xs[dx], zs_at[dz]), (zs_at[dz], ys[dy]))[k]
        return u * 4 + v

    def line_at(k):
        return (z, y, x)[k]

    def remote(src, dst, send, recv, device):
        return pltpu.make_async_remote_copy(
            src_ref=src, dst_ref=dst, send_sem=send, recv_sem=recv, device_id=device, device_id_type=MESH
        )

    pending = []

    def drain():
        for done in pending:
            done()

    items = []
    for layer in (other, mine):
        items.append((q_hbm.at[layer], q.at[layer]))
    for layer in (other, mine):
        items.append((a_hbm.at[layer], a.at[layer]))
        for t in range(512 // TILE):
            items.append((c_hbm.at[layer, pl.ds(t * TILE, TILE)], c.at[layer, pl.ds(t * TILE, TILE)]))
    loads = [pltpu.make_async_copy(s, d, load_sem.at[i]) for i, (s, d) in enumerate(items)]
    for load in loads[:FLY]:
        load.start()

    barrier = pltpu.get_barrier_semaphore()

    pl.semaphore_signal(barrier, inc=1, device_id=sibling, device_id_type=MESH)
    for offset in PLANE + AXIS:
        pl.semaphore_signal(barrier, inc=1, device_id=device(*offset), device_id_type=MESH)

    def arrive(i):
        loads[i].wait()
        if i + FLY < len(loads):
            loads[i + FLY].start()

    for i, layer in enumerate((other, mine)):
        arrive(i)
        q3t[layer] = split3(q[layer]).T
    for n, layer in enumerate((other, mine)):
        base = 2 + n * (1 + 512 // TILE)
        arrive(base)
        for t in range(512 // TILE):
            arrive(base + 1 + t)
            w = dot(c[layer, t * TILE : (t + 1) * TILE, :], q3t[layer], NN)
            wt[:, t * TILE : (t + 1) * TILE] = sum3(w.T) * (1.0 / 32.0)
        part = sum3(dot(split3(wt[...]), a[layer], NN))
        if n == 0:
            for k in range(2):
                px[k][...] = part[:, P_STARTS[k] : P_STARTS[k] + P_WIDTHS[k]]
            pl.semaphore_wait(barrier, 1 + len(PLANE) + len(AXIS))
            p_copies = []
            for k in range(2):
                cp = remote(px[k], pxr[k], core_sem.at[k], corer_sem.at[k], sibling)
                cp.start()
                p_copies.append(cp)
                pending.append(cp.wait_send)
            for offset in AXIS:
                pl.semaphore_signal(near_sem, inc=1, device_id=device(*offset), device_id_type=MESH)

    def all_of(ref, count, send, recv):
        view = ref.at[pl.ds(0, count)]
        return remote(view, view, send, recv, sibling)

    for k in range(2):
        p_copies[k].wait_recv()
        pa[k][first] = part[:, P_STARTS[k] : P_STARTS[k] + P_WIDTHS[k]] + pxr[k][...]
        slot = pa[k].at[first]
        for d, _, _ in AXIS:
            remote(slot, slot, psend_sem.at[k, 0], pa_sem.at[k], along_first(d)).start()
        pending.append(all_of(pa[k], 3, psend_sem.at[k, 0], pa_sem.at[k]).wait_send)
    for k in range(2):
        all_of(pa[k], 3, psend_sem.at[k, 0], pa_sem.at[k]).wait_recv()
        pb[k][second] = pa[k][0] + pa[k][1] + pa[k][2] + pa[k][3]
        slot = pb[k].at[second]
        for d, _, _ in AXIS:
            remote(slot, slot, psend_sem.at[k, 1], pb_sem.at[k], along_second(d)).start()
        pending.append(all_of(pb[k], 3, psend_sem.at[k, 1], pb_sem.at[k]).wait_send)
    for k in range(2):
        all_of(pb[k], 3, psend_sem.at[k, 1], pb_sem.at[k]).wait_recv()
        pf[k][mine] = pb[k][0] + pb[k][1] + pb[k][2] + pb[k][3]
        slot = pf[k].at[mine]
        cp = remote(slot, slot, psend_sem.at[k, 2], pfw_sem.at[k], sibling)
        cp.start()
        pending.append(cp.wait_send)

    def p_pieces(layer):
        return split3(jnp.concatenate([pf[0][layer], pf[1][layer]], axis=1))

    def y_pieces(p3, layer):
        return split3(sum3(dot(p3, a[layer], NT)) * (1.0 / 32.0))

    def gram_of(p3):
        g3 = sum3(dot(p3, p3, NT))
        return g3[:, 0:32] + g3[:, 32:64] + g3[:, 64:96]

    def z_part(y3, layer, k):
        return sum3(dot(y3, c[layer, :, STARTS[k] : STARTS[k] + WIDTHS[k]], NN))

    p3 = p_pieces(mine)
    y3 = y_pieces(p3, mine)
    z_copies = []
    for k in range(3):
        to_pieces(zx[k], z_part(y3, mine, k))
        cp = remote(zx[k], zxr[k], core_sem.at[2 + k], corer_sem.at[2 + k], sibling)
        cp.start()
        z_copies.append(cp)
        pending.append(cp.wait_send)
    g_mine = gram_of(p3)

    for k in range(2):
        slot = pf[k].at[other]
        remote(slot, slot, psend_sem.at[k, 2], pfw_sem.at[k], sibling).wait_recv()
    p3 = p_pieces(other)
    y3 = y_pieces(p3, other)
    for k in range(3):
        to_pieces(zs[k], z_part(y3, other, k))
        z_copies[k].wait_recv()
        zs[k][...] += zxr[k][...]
        if k == 0:
            pl.semaphore_wait(near_sem, len(AXIS))
        me = seat(k, (0, 0, 0))
        for _, du, dv in PLANE:
            offset = spin(k, du, dv, 0)
            remote(
                zs[k].at[seat(k, offset)], zrr[k].at[me], zsend_sem.at[k, 0], zrs_sem.at[k], device(*offset)
            ).start()
        pending.append(all_of(zs[k], 15, zsend_sem.at[k, 0], zrs_sem.at[k]).wait_send)
        zrr[k][me] = zs[k][me]
    g_other = gram_of(p3)
    zero = jnp.zeros((32, 32), F32)
    g_first = jnp.where(core == 0, g_mine, g_other)
    g_second = jnp.where(core == 0, g_other, g_mine)
    gram[z] = jnp.concatenate([g_first, zero, g_second, zero], axis=1)
    for offset in AXIS:
        remote(gram.at[z], gram.at[z], gsend_sem.at[0], g_sem.at[z], device(*offset)).start()
    pending.append(all_of(gram, 3, gsend_sem.at[0], g_sem.at[0]).wait_send)

    for k in range(3):
        all_of(zrr[k], 15, zsend_sem.at[k, 0], zrs_sem.at[k]).wait_recv()
        w = line_at(k)
        zl[k][w] = jnp.sum(zrr[k][...], axis=0)
        for dw, _, _ in AXIS:
            remote(
                zl[k].at[w], zl[k].at[w], zsend_sem.at[k, 1], zline_sem.at[k], device(*spin(k, 0, 0, dw))
            ).start()
        pending.append(all_of(zl[k], 3, zsend_sem.at[k, 1], zline_sem.at[k]).wait_send)
    for k in range(3):
        all_of(zl[k], 3, zsend_sem.at[k, 1], zline_sem.at[k]).wait_recv()
        me = seat(k, (0, 0, 0))
        zag[k][other, me] = zl[k][0] + zl[k][1] + zl[k][2] + zl[k][3]
        own = zag[k].at[other, me]
        for _, du, dv in PLANE:
            remote(own, own, zsend_sem.at[k, 2], zag_sem.at[k, me // 4], device(*spin(k, du, dv, 0))).start()
        pending.append(all_of(zag[k].at[other], 15, zsend_sem.at[k, 2], zag_sem.at[k, 0]).wait_send)

    for offset in AXIS:
        _, from_z = back_from(*offset)
        remote(gram.at[from_z], gram.at[from_z], gsend_sem.at[0], g_sem.at[from_z], sibling).wait_recv()
    inv_ref[...] = invert_factor(gram[0] + gram[1] + gram[2] + gram[3])

    for k in range(3):
        for d in (0, 1, 3, 2):
            u = lax.rem(seat(k, (0, 0, 0)) // 4 + d, 4)
            block = zag[k].at[other, pl.ds(u * 4, 3 if d == 0 else 4)]
            remote(block, block, zsend_sem.at[k, 3], zag_sem.at[k, u], sibling).wait_recv()
            block = zag[k].at[other, pl.ds(u * 4, 4)]
            remote(block, block, zsend_sem.at[k, 3], zfw_sem.at[k], sibling).start()
        pending.append(remote(zag[k].at[other], zag[k].at[other], zsend_sem.at[k, 3], zfw_sem.at[k], sibling).wait_send)
    for k in range(3):
        remote(zag[k].at[mine], zag[k].at[mine], zsend_sem.at[k, 3], zfw_sem.at[k], sibling).wait_recv()
    drain()


def finish_kernel(zag0, zag1, zag2, pf0, pf1, inv_ref, p_out, q_out, *, root):
    for layer in range(2):
        inverse = inv_ref[:, 64 * layer + 32 : 64 * layer + 64]
        pieces = split3(inverse)
        left = jnp.concatenate([pieces, pieces, pieces], axis=1)
        for pf, start, width in zip((pf0, pf1), P_STARTS, P_WIDTHS):
            p_out[layer, :, start : start + width] = sum3(dot(left, split3(pf[layer]), NN)) * root
        for zag, start, width in zip((zag0, zag1, zag2), STARTS, WIDTHS):
            block = from_pieces(zag.at[layer])
            q_out[layer, :, start : start + width] = sum3(dot(left, split3(block), NN))


def local(acts, cotangent, q_start):
    width = cotangent.shape[2]
    q_t = jnp.swapaxes(q_start, 1, 2)
    hbm = pl.BlockSpec(memory_space=pltpu.HBM)
    vmem = pl.BlockSpec(memory_space=pltpu.VMEM)
    dma = pltpu.SemaphoreType.DMA
    *gathered, inverse = pl.pallas_call(
        exchange_kernel,
        out_shape=(
            *[jax.ShapeDtypeStruct((2, 16, 8, width // 4), F32) for width in WIDTHS],
            *[jax.ShapeDtypeStruct((2, 32, width), F32) for width in P_WIDTHS],
            jax.ShapeDtypeStruct((32, 128), F32),
        ),
        in_specs=[hbm] * 3,
        out_specs=(vmem,) * 6,
        scratch_shapes=[
            pltpu.VMEM((2, 512, 1280), BF16),
            pltpu.VMEM((2, 512, 5120), BF16),
            pltpu.VMEM((2, 32, 5120), F32),
            pltpu.VMEM((2, 5120, 96), BF16),
            pltpu.VMEM((32, 512), F32),
            *[pltpu.VMEM((32, width), F32) for _ in range(2) for width in P_WIDTHS],
            *[pltpu.VMEM((4, 32, width), F32) for _ in range(2) for width in P_WIDTHS],
            pltpu.VMEM((4, 32, 128), F32),
            *[pltpu.VMEM((16, 8, width // 4), F32) for _ in range(4) for width in WIDTHS],
            *[pltpu.VMEM((4, 8, width // 4), F32) for width in WIDTHS],
            dma((16,)), dma((5,)), dma((5,)), dma((2, 3)), dma((2,)), dma((2,)), dma((2,)), dma((1,)), dma((4,)),
            dma((3, 4)), dma((3,)), dma((3,)), dma((3, 4)), dma((3,)), pltpu.SemaphoreType.REGULAR,
        ],
        name="exchange",
        compiler_params=pltpu.CompilerParams(
            collective_id=0, has_side_effects=True, vmem_limit_bytes=52 * 2**20
        ),
    )(acts, cotangent, q_t)
    p_t, q_new = pl.pallas_call(
        functools.partial(finish_kernel, root=float(width) ** 0.5),
        out_shape=(
            jax.ShapeDtypeStruct((2, 32, 1280), F32),
            jax.ShapeDtypeStruct((2, 32, 5120), F32),
        ),
        in_specs=[vmem] * 6,
        out_specs=(vmem, vmem),
        name="finish",
        compiler_params=pltpu.CompilerParams(vmem_limit_bytes=32 * 2**20),
    )(*gathered, inverse)
    return jnp.swapaxes(p_t, 1, 2), jnp.swapaxes(q_new, 1, 2)


def solution(mesh):
    placed = (P(None, "dp", "tensor"), P(None, "dp", None), P())
    return jax.shard_map(
        local, mesh=mesh, in_specs=placed, out_specs=(P(None, "tensor", None), P()), check_vma=False
    )
```

time: 49 us -> 48.8 us (level)
  no operation moved by 1% of the time
where the time goes in v5:
time: 48.8 us; the launch traced here: 48.7 us
  Pallas kernels  48.1 us (99%)
  between operations  0.64 us (1%)
    pallas_call x1, Pallas kernels, local(): pl.pallas_call(exchange_kernel, out_shape=(*[jax.ShapeDtypeStruct((2, 16,...  46.2 us
    pallas_call x1, Pallas kernels, local(): pl.pallas_call(functools.partial(finish_kernel, root=float(width) ** 0.5)...  1.95 us

profile of v5, /device:TPU:1, one launch (start us, length us, event | category | flops | bytes accessed | tf_op | source)
XLA Modules:
  0.0 48.7 jit_solution(2335246389843346913)
XLA Ops:
  0.6 46.2 %exchange.1 = (f32[2,16,8,512]{3,2,1,0:T(8,128)S(1)}, f32[2,16,8,384]{3,2,1,0:T(8,128)S(1)}, f32[2,16,8,384]{3,2,1,0:T(8,128)S(1)}, f32[2,32,768]{2,1,0:T(8,128)...) custom-call(bf16[2,512,1280]{2,1,0:T(8,128)(2,1)} %a_hbm.1, bf16[2,512,5120]{2,1,0:T(8,128)(2,1)} %c_hbm.1, ...), custom_call_target="tpu_custom_call" | custom-call | tf_op jit(solution)/shard_map/exchange/pallas_call | solution.py:324
  46.8 1.9 %finish.1 = (f32[2,32,1280]{2,1,0:T(8,128)}, f32[2,32,5120]{2,1,0:T(8,128)}) custom-call(f32[2,16,8,512]{3,2,1,0:T(8,128)S(1)} %get-tuple-element.10.zag0, f32[2,16,8,384]{3,2,1,0:T(8,128)S(1)} %get-tuple-element.11.zag1, f32[2,16,8,384]{3,2,1,0:T(8,128)S(1)} %get-tuple-element.12.zag2, f32[2,32,768]{2,1,0:T(8,128)S(1)} %get-tuple-element.13.pf0, ...), custom_call_target="tpu_custom_call" | custom-call | tf_op jit(solution)/shard_map/finish/pallas_call | solution.py:352

commit v6 on v5

v6 whole, which is shorter than its diff:
```python
import functools

import jax
import jax.numpy as jnp
from jax import lax
from jax.experimental import pallas as pl
from jax.experimental.pallas import tpu as pltpu
from jax.sharding import PartitionSpec as P

MESH = pl.DeviceIdType.MESH
F32 = jnp.float32
BF16 = jnp.bfloat16
NN = (((1,), (0,)), ((), ()))
NT = (((1,), (1,)), ((), ()))
TILE = 256
FLY = 5
WIDTHS = (1024, 1024, 512)
P_WIDTHS = (384, 256)
STARTS = tuple(sum(WIDTHS[:k]) for k in range(len(WIDTHS)))
P_STARTS = tuple(sum(P_WIDTHS[:k]) for k in range(len(P_WIDTHS)))
Z_CHUNKS, P_CHUNKS = len(WIDTHS), len(P_WIDTHS)
Z_HALF, P_HALF = sum(WIDTHS), sum(P_WIDTHS)


def hops(offset):
    return sum(min(d, 4 - d) for d in offset)


OFFSETS = [(dz, dy, dx) for dz in range(4) for dy in range(4) for dx in range(4)]
CUBE = sorted([o for o in OFFSETS if hops(o) > 0], key=hops, reverse=True)
PLANE = [o for o in CUBE if o[0] == 0]
AXIS = [o for o in CUBE if o[1] == 0 and o[2] == 0]
FLY = 5


def dot(a, b, dims):
    return lax.dot_general(a, b, dims, preferred_element_type=F32)


def split3(x):
    hi = x.astype(BF16)
    rest = x - hi.astype(F32)
    mid = rest.astype(BF16)
    low = (rest - mid.astype(F32)).astype(BF16)
    return jnp.concatenate([hi, mid, low], axis=0)


def sum3(x):
    return x[0:32] + x[32:64] + x[64:96]


def to_pieces(ref, value):
    quarter = value.shape[1] // 4
    for j in range(16):
        g, h = j // 4, j % 4
        ref[j] = value[8 * g : 8 * g + 8, quarter * h : quarter * h + quarter]


def from_pieces(ref):
    bands = []
    for g in range(4):
        bands.append(jnp.concatenate([ref[4 * g + h] for h in range(4)], axis=1))
    return jnp.concatenate(bands, axis=0)


def invert_factor(grams):
    rows = lax.broadcasted_iota(jnp.int32, (32, 128), 0)
    lanes = lax.broadcasted_iota(jnp.int32, (32, 128), 1)
    eye = jnp.where(rows == lanes % 32, 1.0, 0.0).astype(F32)
    work = jnp.where((lanes // 32) % 2 == 1, eye, grams)
    first = lanes < 64
    for k in range(32):
        row = work[k : k + 1, :]
        pivot = jnp.where(first[0:1], row[:, k : k + 1], row[:, 64 + k : 65 + k])
        scale = lax.rsqrt(pivot)
        scale = scale * (1.5 - 0.5 * pivot * scale * scale)
        column = jnp.where(first, work[:, k : k + 1], work[:, 64 + k : 65 + k])
        row = row * scale
        work = jnp.where(rows > k, work - (column * scale) * row, jnp.where(rows == k, row, work))
    return work


def exchange_kernel(a_hbm, c_hbm, q_hbm, *refs):
    left = list(refs)

    def take(count):
        taken = left[:count]
        del left[:count]
        return taken

    zag, pf = [take(Z_CHUNKS) for _ in range(2)], [take(P_CHUNKS) for _ in range(2)]
    (inv_ref,) = take(1)
    a, c, q, q3t, wt, px, pxr, gram = take(8)
    pa, pb = ([take(P_CHUNKS) for _ in range(2)] for _ in range(2))
    zx, zxr, zs, zrr, zl = ([take(Z_CHUNKS) for _ in range(2)] for _ in range(5))
    load_sem, px_sem, pxr_sem, psend_sem, pa_sem, pb_sem, pfw_sem, gsend_sem, g_sem = take(9)
    zx_sem, zxr_sem, zsend_sem, zrs_sem, zline_sem, zag_sem, zfw_sem, near_sem = take(8)
    dp = lax.axis_index("dp")
    z = lax.axis_index("tensor")
    core = lax.rem(dp, 2)
    plane = dp // 2
    y, x = plane // 4, lax.rem(plane, 4)
    mine, other = core, 1 - core
    sibling = {"dp": plane * 2 + other, "tensor": z}

    ys = [lax.rem(y + d, 4) for d in range(4)]
    xs = [lax.rem(x + d, 4) for d in range(4)]
    zs_at = [lax.rem(z + d, 4) for d in range(4)]

    def place(dz, dy, dx):
        return ys[dy] * 4 + xs[dx], zs_at[dz]

    def device(dz, dy, dx):
        to_plane, to_z = place(dz, dy, dx)
        return {"dp": to_plane * 2 + core, "tensor": to_z}

    def back_from(dz, dy, dx):
        return place((4 - dz) % 4, (4 - dy) % 4, (4 - dx) % 4)

    first, second = jnp.where(core == 0, x, y), jnp.where(core == 0, y, x)

    def along_first(d):
        row, column = jnp.where(core == 0, y, ys[d]), jnp.where(core == 0, xs[d], x)
        return {"dp": (row * 4 + column) * 2 + core, "tensor": z}

    def along_second(d):
        row, column = jnp.where(core == 0, ys[d], y), jnp.where(core == 0, x, xs[d])
        return {"dp": (row * 4 + column) * 2 + core, "tensor": z}

    def spin(l, k, du, dv, dw):
        return ((dw, du, dv), (dv, dw, du), (du, dv, dw))[(l + k) % 3]

    def seat(l, k, offset):
        dz, dy, dx = offset
        u, v = ((ys[dy], xs[dx]), (xs[dx], zs_at[dz]), (zs_at[dz], ys[dy]))[(l + k) % 3]
        return u * 4 + v

    def line_at(l, k):
        return (z, y, x)[(l + k) % 3]

    def remote(src, dst, send, recv, device):
        return pltpu.make_async_remote_copy(
            src_ref=src, dst_ref=dst, send_sem=send, recv_sem=recv, device_id=device, device_id_type=MESH
        )

    pending = []

    def drain():
        for done in pending:
            done()

    def all_of(ref, count, send, recv):
        view = ref.at[pl.ds(0, count)]
        return remote(view, view, send, recv, sibling)

    items = []
    for l in range(2):
        items.append((q_hbm.at[l], q.at[l]))
    for l in range(2):
        items.append((a_hbm.at[l], a.at[l]))
        for t in range(512 // TILE):
            items.append((c_hbm.at[l, pl.ds(t * TILE, TILE)], c.at[l, pl.ds(t * TILE, TILE)]))
    loads = [pltpu.make_async_copy(s, d, load_sem.at[i]) for i, (s, d) in enumerate(items)]
    for load in loads[:FLY]:
        load.start()

    barrier = pltpu.get_barrier_semaphore()

    pl.semaphore_signal(barrier, inc=1, device_id=sibling, device_id_type=MESH)
    for offset in PLANE + AXIS:
        pl.semaphore_signal(barrier, inc=1, device_id=device(*offset), device_id_type=MESH)

    def arrive(i):
        loads[i].wait()
        if i + FLY < len(loads):
            loads[i + FLY].start()

    def half_of(h):
        return pl.ds(pl.multiple_of(h * P_HALF, 128), P_HALF)

    def tokens(l, t):
        base = 2 + l * (1 + 512 // TILE)
        if t == 0:
            arrive(base)
        arrive(base + 1 + t)
        w = dot(c[l, t * TILE : (t + 1) * TILE, :], q3t[l], NN)
        wt[:, t * TILE : (t + 1) * TILE] = sum3(w.T) * (1.0 / 32.0)

    def p_part(l, h):
        return sum3(dot(split3(wt[...]), a[l, :, half_of(h)], NN))

    def pair_start(l):
        px[l] = p_part(l, other)
        cp = remote(px.at[l], pxr.at[l], px_sem.at[l], pxr_sem.at[l], sibling)
        cp.start()
        pending.append(cp.wait_send)
        return p_part(l, mine)

    def p_first(l, part):
        remote(px.at[l], pxr.at[l], px_sem.at[l], pxr_sem.at[l], sibling).wait_recv()
        for k in range(P_CHUNKS):
            cols = slice(P_STARTS[k], P_STARTS[k] + P_WIDTHS[k])
            pa[l][k][first] = part[:, cols] + pxr[l, :, cols]
            slot = pa[l][k].at[first]
            for d, _, _ in AXIS:
                remote(slot, slot, psend_sem.at[l, k, 0], pa_sem.at[l, k], along_first(d)).start()
            pending.append(all_of(pa[l][k], 3, psend_sem.at[l, k, 0], pa_sem.at[l, k]).wait_send)

    def p_second(l):
        for k in range(P_CHUNKS):
            src, dst = pa[l][k], pb[l][k]
            all_of(src, 3, psend_sem.at[l, k, 0], pa_sem.at[l, k]).wait_recv()
            dst[second] = src[0] + src[1] + src[2] + src[3]
            slot = dst.at[second]
            for d, _, _ in AXIS:
                remote(slot, slot, psend_sem.at[l, k, 1], pb_sem.at[l, k], along_second(d)).start()
            pending.append(all_of(dst, 3, psend_sem.at[l, k, 1], pb_sem.at[l, k]).wait_send)

    def p_third(l):
        for k in range(P_CHUNKS):
            src = pb[l][k]
            all_of(src, 3, psend_sem.at[l, k, 1], pb_sem.at[l, k]).wait_recv()
            pf[l][k][mine] = src[0] + src[1] + src[2] + src[3]
            slot = pf[l][k].at[mine]
            cp = remote(slot, slot, psend_sem.at[l, k, 2], pfw_sem.at[l, k], sibling)
            cp.start()
            pending.append(cp.wait_send)

    def half_pieces(l, h):
        return split3(jnp.concatenate([pf[l][k][h] for k in range(P_CHUNKS)], axis=1))

    def gram_of(p3):
        g3 = sum3(dot(p3, p3, NT))
        return g3[:, 0:32] + g3[:, 32:64] + g3[:, 64:96]

    def y_pieces(l):
        p_mine = half_pieces(l, mine)
        y = sum3(dot(p_mine, a[l, :, half_of(mine)], NT))
        for k in range(P_CHUNKS):
            slot = pf[l][k].at[other]
            remote(slot, slot, psend_sem.at[l, k, 2], pfw_sem.at[l, k], sibling).wait_recv()
        p_other = half_pieces(l, other)
        y = y + sum3(dot(p_other, a[l, :, half_of(other)], NT))
        return split3(y * (1.0 / 32.0)), p_mine, p_other

    def z_part(l, k, h, y3):
        cols = pl.ds(pl.multiple_of(h * Z_HALF + STARTS[k], 128), WIDTHS[k])
        return sum3(dot(y3, c[l, :, cols], NN))

    def z_scatter(l, y3):
        for k in range(Z_CHUNKS):
            to_pieces(zx[l][k], z_part(l, k, other, y3))
            cp = remote(zx[l][k], zxr[l][k], zx_sem.at[l, k], zxr_sem.at[l, k], sibling)
            cp.start()
            pending.append(cp.wait_send)
        for k in range(Z_CHUNKS):
            to_pieces(zs[l][k], z_part(l, k, mine, y3))
            remote(zx[l][k], zxr[l][k], zx_sem.at[l, k], zxr_sem.at[l, k], sibling).wait_recv()
            zs[l][k][...] += zxr[l][k][...]
            me = seat(l, k, (0, 0, 0))
            for _, du, dv in PLANE:
                offset = spin(l, k, du, dv, 0)
                remote(
                    zs[l][k].at[seat(l, k, offset)], zrr[l][k].at[me],
                    zsend_sem.at[l, k, 0], zrs_sem.at[l, k], device(*offset),
                ).start()
            pending.append(all_of(zs[l][k], 15, zsend_sem.at[l, k, 0], zrs_sem.at[l, k]).wait_send)
            zrr[l][k][me] = zs[l][k][me]

    def z_line(l):
        for k in range(Z_CHUNKS):
            all_of(zrr[l][k], 15, zsend_sem.at[l, k, 0], zrs_sem.at[l, k]).wait_recv()
            w = line_at(l, k)
            zl[l][k][w] = jnp.sum(zrr[l][k][...], axis=0)
            slot = zl[l][k].at[w]
            for dw, _, _ in AXIS:
                remote(
                    slot, slot, zsend_sem.at[l, k, 1], zline_sem.at[l, k], device(*spin(l, k, 0, 0, dw))
                ).start()
            pending.append(all_of(zl[l][k], 3, zsend_sem.at[l, k, 1], zline_sem.at[l, k]).wait_send)

    def z_gather(l):
        for k in range(Z_CHUNKS):
            src = zl[l][k]
            all_of(src, 3, zsend_sem.at[l, k, 1], zline_sem.at[l, k]).wait_recv()
            me = seat(l, k, (0, 0, 0))
            zag[l][k][mine, me] = src[0] + src[1] + src[2] + src[3]
            own = zag[l][k].at[mine, me]
            for _, du, dv in PLANE:
                remote(
                    own, own, zsend_sem.at[l, k, 2], zag_sem.at[l, k, me // 4], device(*spin(l, k, du, dv, 0))
                ).start()
            pending.append(all_of(zag[l][k].at[mine], 15, zsend_sem.at[l, k, 2], zag_sem.at[l, k, 0]).wait_send)

    def z_forward(l):
        for k in range(Z_CHUNKS):
            whole = zag[l][k].at[mine]
            for d in (0, 1, 3, 2):
                u = lax.rem(seat(l, k, (0, 0, 0)) // 4 + d, 4)
                block = zag[l][k].at[mine, pl.ds(u * 4, 3 if d == 0 else 4)]
                remote(block, block, zsend_sem.at[l, k, 3], zag_sem.at[l, k, u], sibling).wait_recv()
                block = zag[l][k].at[mine, pl.ds(u * 4, 4)]
                remote(block, block, zsend_sem.at[l, k, 3], zfw_sem.at[l, k], sibling).start()
            pending.append(remote(whole, whole, zsend_sem.at[l, k, 3], zfw_sem.at[l, k], sibling).wait_send)

    def z_finish(l):
        for k in range(Z_CHUNKS):
            whole = zag[l][k].at[other]
            remote(whole, whole, zsend_sem.at[l, k, 3], zfw_sem.at[l, k], sibling).wait_recv()

    for l in range(2):
        arrive(l)
        q3t[l] = split3(q[l]).T
    for t in range(512 // TILE):
        tokens(0, t)
    pl.semaphore_wait(barrier, 1 + len(PLANE) + len(AXIS))
    for offset in AXIS:
        pl.semaphore_signal(near_sem, inc=1, device_id=device(*offset), device_id_type=MESH)
    part = pair_start(0)
    tokens(1, 0)
    p_first(0, part)
    for t in range(1, 512 // TILE):
        tokens(1, t)
    part = pair_start(1)
    p_first(1, part)
    p_second(0)
    p_second(1)
    pl.semaphore_wait(near_sem, len(AXIS))
    p_third(0)
    y3, p_mine, p_other = y_pieces(0)
    z_scatter(0, y3)
    g_first = gram_of(p_mine) + gram_of(p_other)
    p_third(1)
    y3, p_mine, p_other = y_pieces(1)
    z_scatter(1, y3)
    g_second = gram_of(p_mine) + gram_of(p_other)
    zero = jnp.zeros((32, 32), F32)
    gram[z] = jnp.concatenate([g_first, zero, g_second, zero], axis=1)
    for offset in AXIS:
        remote(gram.at[z], gram.at[z], gsend_sem.at[0], g_sem.at[z], device(*offset)).start()
    pending.append(all_of(gram, 3, gsend_sem.at[0], g_sem.at[0]).wait_send)
    z_line(0)
    z_gather(0)
    z_line(1)
    for offset in AXIS:
        _, from_z = back_from(*offset)
        remote(gram.at[from_z], gram.at[from_z], gsend_sem.at[0], g_sem.at[from_z], sibling).wait_recv()
    inv_ref[...] = invert_factor(gram[0] + gram[1] + gram[2] + gram[3])
    z_gather(1)
    z_forward(0)
    z_forward(1)
    z_finish(0)
    z_finish(1)
    drain()


def finish_kernel(*refs, root):
    zags, pfs = refs[: 2 * Z_CHUNKS], refs[2 * Z_CHUNKS : 2 * Z_CHUNKS + 2 * P_CHUNKS]
    inv_ref, p_out, q_out = refs[2 * Z_CHUNKS + 2 * P_CHUNKS :]
    for l in range(2):
        pieces = split3(inv_ref[:, 64 * l + 32 : 64 * l + 64])
        left = jnp.concatenate([pieces, pieces, pieces], axis=1)
        for h in range(2):
            for k in range(P_CHUNKS):
                start = h * P_HALF + P_STARTS[k]
                block = pfs[l * P_CHUNKS + k][h]
                p_out[l, :, start : start + P_WIDTHS[k]] = sum3(dot(left, split3(block), NN)) * root
            for k in range(Z_CHUNKS):
                start = h * Z_HALF + STARTS[k]
                block = from_pieces(zags[l * Z_CHUNKS + k].at[h])
                q_out[l, :, start : start + WIDTHS[k]] = sum3(dot(left, split3(block), NN))


def local(acts, cotangent, q_start):
    width = cotangent.shape[2]
    q_t = jnp.swapaxes(q_start, 1, 2)
    hbm = pl.BlockSpec(memory_space=pltpu.HBM)
    vmem = pl.BlockSpec(memory_space=pltpu.VMEM)
    dma = pltpu.SemaphoreType.DMA
    count = 2 * Z_CHUNKS + 2 * P_CHUNKS + 1

    def chunks(shape_of, widths, times=1):
        return [pltpu.VMEM(shape_of(width), F32) for _ in range(2 * times) for width in widths]

    *gathered, inverse = pl.pallas_call(
        exchange_kernel,
        out_shape=(
            *[jax.ShapeDtypeStruct((2, 16, 8, w // 4), F32) for _ in range(2) for w in WIDTHS],
            *[jax.ShapeDtypeStruct((2, 32, w), F32) for _ in range(2) for w in P_WIDTHS],
            jax.ShapeDtypeStruct((32, 128), F32),
        ),
        in_specs=[hbm] * 3,
        out_specs=(vmem,) * count,
        scratch_shapes=[
            pltpu.VMEM((2, 512, 1280), BF16),
            pltpu.VMEM((2, 512, 5120), BF16),
            pltpu.VMEM((2, 32, 5120), F32),
            pltpu.VMEM((2, 5120, 96), BF16),
            pltpu.VMEM((32, 512), F32),
            pltpu.VMEM((2, 32, P_HALF), F32),
            pltpu.VMEM((2, 32, P_HALF), F32),
            pltpu.VMEM((4, 32, 128), F32),
            *chunks(lambda w: (4, 32, w), P_WIDTHS, 2),
            *chunks(lambda w: (16, 8, w // 4), WIDTHS, 4),
            *chunks(lambda w: (4, 8, w // 4), WIDTHS),
            dma((16,)), dma((2,)), dma((2,)), dma((2, P_CHUNKS, 3)), dma((2, P_CHUNKS)), dma((2, P_CHUNKS)),
            dma((2, P_CHUNKS)), dma((1,)), dma((4,)),
            dma((2, Z_CHUNKS)), dma((2, Z_CHUNKS)), dma((2, Z_CHUNKS, 4)), dma((2, Z_CHUNKS)), dma((2, Z_CHUNKS)),
            dma((2, Z_CHUNKS, 4)), dma((2, Z_CHUNKS)), pltpu.SemaphoreType.REGULAR,
        ],
        name="exchange",
        compiler_params=pltpu.CompilerParams(
            collective_id=0, has_side_effects=True, vmem_limit_bytes=52 * 2**20
        ),
    )(acts, cotangent, q_t)
    p_t, q_new = pl.pallas_call(
        functools.partial(finish_kernel, root=float(width) ** 0.5),
        out_shape=(
            jax.ShapeDtypeStruct((2, 32, 1280), F32),
            jax.ShapeDtypeStruct((2, 32, 5120), F32),
        ),
        in_specs=[vmem] * count,
        out_specs=(vmem, vmem),
        name="finish",
        compiler_params=pltpu.CompilerParams(vmem_limit_bytes=32 * 2**20),
    )(*gathered, inverse)
    return jnp.swapaxes(p_t, 1, 2), jnp.swapaxes(q_new, 1, 2)


def solution(mesh):
    placed = (P(None, "dp", "tensor"), P(None, "dp", None), P())
    return jax.shard_map(
        local, mesh=mesh, in_specs=placed, out_specs=(P(None, "tensor", None), P()), check_vma=False
    )
```

time: 48.8 us -> 48.8 us (level)
  no operation moved by 1% of the time
where the time goes in v6:
time: 48.8 us; the launch traced here: 48.7 us
  Pallas kernels  48.1 us (99%)
  between operations  0.64 us (1%)
    pallas_call x1, Pallas kernels, local(): pl.pallas_call(exchange_kernel, out_shape=(*[jax.ShapeDtypeStruct((2, 16,...  46.1 us
    pallas_call x1, Pallas kernels, local(): pl.pallas_call(functools.partial(finish_kernel, root=float(width) ** 0.5)...  1.93 us

profile of v6, /device:TPU:1, one launch (start us, length us, event | category | flops | bytes accessed | tf_op | source)
XLA Modules:
  0.0 48.7 jit_solution(10267282523599568470)
XLA Ops:
  0.6 46.1 %exchange.1 = (f32[2,16,8,256]{3,2,1,0:T(8,128)S(1)}, f32[2,16,8,256]{3,2,1,0:T(8,128)S(1)}, f32[2,16,8,128]{3,2,1,0:T(8,128)S(1)}, f32[2,16,8,256]{3,2,1,0:T(8,...) custom-call(bf16[2,512,1280]{2,1,0:T(8,128)(2,1)} %a_hbm.1, ...), custom_call_target="tpu_custom_call" | custom-call | tf_op jit(solution)/shard_map/exchange/pallas_call | solution.py:385
  46.8 1.9 %finish.1 = (f32[2,32,1280]{2,1,0:T(8,128)}, f32[2,32,5120]{2,1,0:T(8,128)}) custom-call(f32[2,16,8,256]{3,2,1,0:T(8,128)S(1)} %get-tuple-element.15.refs_0_, f32[2,16,8,256]{3,2,1,0:T(8,128)S(1)} %get-tuple-element.16.refs_1_, f32[2,16,8,128]{3,2,1,0:T(8,128)S(1)} %get-tuple-element.17.refs_2_, f32[2,16,8,256]{3,2,1,0:T(8,128)S(1)} %get-tuple-element.18.refs_3_, ...), custom_call_target="tpu_custom_call" | custom-call | tf_op jit(solution)/shard_map/finish/pallas_call | solution.py:416

commit v7 on v6

--- a/solution.py
+++ b/solution.py
@@ -63,13 +63,14 @@
     return jnp.concatenate(bands, axis=0)
 
 
-def invert_factor(grams):
+def eliminate(work, steps, start=False):
     rows = lax.broadcasted_iota(jnp.int32, (32, 128), 0)
     lanes = lax.broadcasted_iota(jnp.int32, (32, 128), 1)
-    eye = jnp.where(rows == lanes % 32, 1.0, 0.0).astype(F32)
-    work = jnp.where((lanes // 32) % 2 == 1, eye, grams)
+    if start:
+        eye = jnp.where(rows == lanes % 32, 1.0, 0.0).astype(F32)
+        work = jnp.where((lanes // 32) % 2 == 1, eye, work)
     first = lanes < 64
-    for k in range(32):
+    for k in steps:
         row = work[k : k + 1, :]
         pivot = jnp.where(first[0:1], row[:, k : k + 1], row[:, 64 + k : 65 + k])
         scale = lax.rsqrt(pivot)
@@ -340,13 +341,13 @@
         remote(gram.at[z], gram.at[z], gsend_sem.at[0], g_sem.at[z], device(*offset)).start()
     pending.append(all_of(gram, 3, gsend_sem.at[0], g_sem.at[0]).wait_send)
     z_line(0)
+    z_line(1)
     z_gather(0)
-    z_line(1)
+    z_gather(1)
     for offset in AXIS:
         _, from_z = back_from(*offset)
         remote(gram.at[from_z], gram.at[from_z], gsend_sem.at[0], g_sem.at[from_z], sibling).wait_recv()
-    inv_ref[...] = invert_factor(gram[0] + gram[1] + gram[2] + gram[3])
-    z_gather(1)
+    inv_ref[...] = eliminate(gram[0] + gram[1] + gram[2] + gram[3], range(32), True)
     z_forward(0)
     z_forward(1)
     z_finish(0)

time: 48.8 us -> 46.9 us (0.961)
  Pallas kernels: 48.1 us -> 46.2 us
    pallas_call x1, Pallas kernels: 46.1 us -> 44.2 us  [local(): pl.pallas_call(exchange_kernel, out_shape=(*[jax.ShapeDtypeStruct((2, 16,...]
where the time goes in v7:
time: 46.9 us; the launch traced here: 46.8 us
  Pallas kernels  46.2 us (99%)
  between operations  0.64 us (1%)
    pallas_call x1, Pallas kernels, local(): pl.pallas_call(exchange_kernel, out_shape=(*[jax.ShapeDtypeStruct((2, 16,...  44.2 us
    pallas_call x1, Pallas kernels, local(): pl.pallas_call(functools.partial(finish_kernel, root=float(width) ** 0.5)...  1.92 us

profile of v7, /device:TPU:1, one launch (start us, length us, event | category | flops | bytes accessed | tf_op | source)
XLA Modules:
  0.0 46.8 jit_solution(12643701250244736401)
XLA Ops:
  0.6 44.2 %exchange.1 = (f32[2,16,8,256]{3,2,1,0:T(8,128)S(1)}, f32[2,16,8,256]{3,2,1,0:T(8,128)S(1)}, f32[2,16,8,128]{3,2,1,0:T(8,128)S(1)}, f32[2,16,8,256]{3,2,1,0:T(8,...) custom-call(bf16[2,512,1280]{2,1,0:T(8,128)(2,1)} %a_hbm.1, ...), custom_call_target="tpu_custom_call" | custom-call | tf_op jit(solution)/shard_map/exchange/pallas_call | solution.py:386
  44.9 1.9 %finish.1 = (f32[2,32,1280]{2,1,0:T(8,128)}, f32[2,32,5120]{2,1,0:T(8,128)}) custom-call(f32[2,16,8,256]{3,2,1,0:T(8,128)S(1)} %get-tuple-element.15.refs_0_, f32[2,16,8,256]{3,2,1,0:T(8,128)S(1)} %get-tuple-element.16.refs_1_, f32[2,16,8,128]{3,2,1,0:T(8,128)S(1)} %get-tuple-element.17.refs_2_, f32[2,16,8,256]{3,2,1,0:T(8,128)S(1)} %get-tuple-element.18.refs_3_, ...), custom_call_target="tpu_custom_call" | custom-call | tf_op jit(solution)/shard_map/finish/pallas_call | solution.py:417

commit v8 on v7

--- a/solution.py
+++ b/solution.py
@@ -81,7 +81,12 @@
     return work
 
 
-def exchange_kernel(a_hbm, c_hbm, q_hbm, *refs):
+def factor(inv_ref, l):
+    pieces = split3(inv_ref[:, 64 * l + 32 : 64 * l + 64])
+    return jnp.concatenate([pieces, pieces, pieces], axis=1)
+
+
+def exchange_kernel(a_hbm, c_hbm, q_hbm, *refs, root):
     left = list(refs)
 
     def take(count):
@@ -89,8 +94,10 @@
         del left[:count]
         return taken
 
-    zag, pf = [take(Z_CHUNKS) for _ in range(2)], [take(P_CHUNKS) for _ in range(2)]
+    q_done, p_done = take(2)
+    late = take(Z_CHUNKS)
     (inv_ref,) = take(1)
+    zag, pf = [take(Z_CHUNKS), late], [take(P_CHUNKS) for _ in range(2)]
     a, c, q, q3t, wt, px, pxr, gram = take(8)
     pa, pb = ([take(P_CHUNKS) for _ in range(2)] for _ in range(2))
     zx, zxr, zs, zrr, zl = ([take(Z_CHUNKS) for _ in range(2)] for _ in range(5))
@@ -348,28 +355,49 @@
         _, from_z = back_from(*offset)
         remote(gram.at[from_z], gram.at[from_z], gsend_sem.at[0], g_sem.at[from_z], sibling).wait_recv()
     inv_ref[...] = eliminate(gram[0] + gram[1] + gram[2] + gram[3], range(32), True)
-    z_forward(0)
-    z_forward(1)
-    z_finish(0)
-    z_finish(1)
-    drain()
-
-
-def finish_kernel(*refs, root):
-    zags, pfs = refs[: 2 * Z_CHUNKS], refs[2 * Z_CHUNKS : 2 * Z_CHUNKS + 2 * P_CHUNKS]
-    inv_ref, p_out, q_out = refs[2 * Z_CHUNKS + 2 * P_CHUNKS :]
+    inverse = [factor(inv_ref, l) for l in range(2)]
+
+    def q_half(l, h):
+        for k in range(Z_CHUNKS):
+            cols = pl.ds(pl.multiple_of(h * Z_HALF + STARTS[k], 128), WIDTHS[k])
+            q_done[l, :, cols] = sum3(dot(inverse[l], split3(from_pieces(zag[l][k].at[h])), NN))
+
     for l in range(2):
-        pieces = split3(inv_ref[:, 64 * l + 32 : 64 * l + 64])
-        left = jnp.concatenate([pieces, pieces, pieces], axis=1)
         for h in range(2):
             for k in range(P_CHUNKS):
                 start = h * P_HALF + P_STARTS[k]
-                block = pfs[l * P_CHUNKS + k][h]
-                p_out[l, :, start : start + P_WIDTHS[k]] = sum3(dot(left, split3(block), NN)) * root
-            for k in range(Z_CHUNKS):
-                start = h * Z_HALF + STARTS[k]
-                block = from_pieces(zags[l * Z_CHUNKS + k].at[h])
-                q_out[l, :, start : start + WIDTHS[k]] = sum3(dot(left, split3(block), NN))
+                p_done[l, :, start : start + P_WIDTHS[k]] = sum3(dot(inverse[l], split3(pf[l][k][h]), NN)) * root
+    z_forward(0)
+    q_half(0, mine)
+    z_finish(0)
+    q_half(0, other)
+    z_forward(1)
+    q_half(1, mine)
+    z_finish(1)
+    drain()
+
+
+def finish_kernel(q_done, p_done, *refs):
+    late, (inv_ref, p_out, q_out, last, sem) = refs[:Z_CHUNKS], refs[Z_CHUNKS:]
+    mine = lax.rem(lax.axis_index("dp"), 2)
+    other = 1 - mine
+    own = pl.ds(pl.multiple_of(mine * Z_HALF, 128), Z_HALF)
+    rest = pl.ds(pl.multiple_of(other * Z_HALF, 128), Z_HALF)
+    copies = [
+        pltpu.make_async_copy(q_done.at[0], q_out.at[0], sem.at[0]),
+        pltpu.make_async_copy(q_done.at[1, :, own], q_out.at[1, :, own], sem.at[1]),
+        pltpu.make_async_copy(p_done, p_out, sem.at[2]),
+    ]
+    for cp in copies:
+        cp.start()
+    inverse = factor(inv_ref, 1)
+    for k in range(Z_CHUNKS):
+        block = from_pieces(late[k].at[other])
+        last[:, STARTS[k] : STARTS[k] + WIDTHS[k]] = sum3(dot(inverse, split3(block), NN))
+    copies.append(pltpu.make_async_copy(last, q_out.at[1, :, rest], sem.at[3]))
+    copies[3].start()
+    for cp in copies:
+        cp.wait()
 
 
 def local(acts, cotangent, q_start):
@@ -378,21 +406,24 @@
     hbm = pl.BlockSpec(memory_space=pltpu.HBM)
     vmem = pl.BlockSpec(memory_space=pltpu.VMEM)
     dma = pltpu.SemaphoreType.DMA
-    count = 2 * Z_CHUNKS + 2 * P_CHUNKS + 1
+    count = Z_CHUNKS + 3
 
     def chunks(shape_of, widths, times=1):
         return [pltpu.VMEM(shape_of(width), F32) for _ in range(2 * times) for width in widths]
 
-    *gathered, inverse = pl.pallas_call(
-        exchange_kernel,
+    finished = pl.pallas_call(
+        functools.partial(exchange_kernel, root=float(width) ** 0.5),
         out_shape=(
-            *[jax.ShapeDtypeStruct((2, 16, 8, w // 4), F32) for _ in range(2) for w in WIDTHS],
-            *[jax.ShapeDtypeStruct((2, 32, w), F32) for _ in range(2) for w in P_WIDTHS],
+            jax.ShapeDtypeStruct((2, 32, 2 * Z_HALF), F32),
+            jax.ShapeDtypeStruct((2, 32, 2 * P_HALF), F32),
+            *[jax.ShapeDtypeStruct((2, 16, 8, w // 4), F32) for w in WIDTHS],
             jax.ShapeDtypeStruct((32, 128), F32),
         ),
         in_specs=[hbm] * 3,
         out_specs=(vmem,) * count,
         scratch_shapes=[
+            *[pltpu.VMEM((2, 16, 8, w // 4), F32) for w in WIDTHS],
+            *chunks(lambda w: (2, 32, w), P_WIDTHS),
             pltpu.VMEM((2, 512, 1280), BF16),
             pltpu.VMEM((2, 512, 5120), BF16),
             pltpu.VMEM((2, 32, 5120), F32),
@@ -411,20 +442,21 @@
         ],
         name="exchange",
         compiler_params=pltpu.CompilerParams(
-            collective_id=0, has_side_effects=True, vmem_limit_bytes=52 * 2**20
+            collective_id=0, has_side_effects=True, vmem_limit_bytes=51 * 2**20
         ),
     )(acts, cotangent, q_t)
     p_t, q_new = pl.pallas_call(
-        functools.partial(finish_kernel, root=float(width) ** 0.5),
+        finish_kernel,
         out_shape=(
-            jax.ShapeDtypeStruct((2, 32, 1280), F32),
-            jax.ShapeDtypeStruct((2, 32, 5120), F32),
+            jax.ShapeDtypeStruct((2, 32, 2 * P_HALF), F32),
+            jax.ShapeDtypeStruct((2, 32, 2 * Z_HALF), F32),
         ),
         in_specs=[vmem] * count,
-        out_specs=(vmem, vmem),
+        out_specs=(hbm, hbm),
+        scratch_shapes=[pltpu.VMEM((32, Z_HALF), F32), dma((4,))],
         name="finish",
         compiler_params=pltpu.CompilerParams(vmem_limit_bytes=32 * 2**20),
-    )(*gathered, inverse)
+    )(*finished)
     return jnp.swapaxes(p_t, 1, 2), jnp.swapaxes(q_new, 1, 2)
 
 

time: 46.9 us -> 46.2 us (0.985)
  Pallas kernels: 46.2 us -> 45.4 us
    pallas_call x2, Pallas kernels: 46.2 us -> 45.4 us  [the longest x1 44.2 us: local(): pl.pallas_call(functools.partial(exchange_kernel, root=float(width) ** 0....]
where the time goes in v8:
time: 46.2 us; the launch traced here: 46.1 us
  Pallas kernels  45.4 us (98%)
  between operations  0.64 us (1%)
    pallas_call x1, Pallas kernels, local(): pl.pallas_call(functools.partial(exchange_kernel, root=float(width) ** 0....  44.2 us
    pallas_call x1, Pallas kernels, local(): pl.pallas_call(finish_kernel, out_shape=(jax.ShapeDtypeStruct((2, 32, 2 *...  1.2 us

profile of v8, /device:TPU:1, one launch (start us, length us, event | category | flops | bytes accessed | tf_op | source)
XLA Modules:
  0.0 46.1 jit_solution(4286135226127628600)
XLA Ops:
  0.6 44.2 %exchange.1 = (f32[2,32,5120]{2,1,0:T(8,128)S(1)}, f32[2,32,1280]{2,1,0:T(8,128)S(1)}, f32[2,16,8,256]{3,2,1,0:T(8,128)S(1)}, f32[2,16,8,256]{3,2,1,0:T(8,128)S(...) custom-call(bf16[2,512,1280]{2,1,0:T(8,128)(2,1)} %a_hbm.1, bf16[2,512,5120]{2,1,0:T(8,128)(2,1)} %c_hbm.1, ...), custom_call_target="tpu_custom_call" | custom-call | tf_op jit(solution)/shard_map/exchange/pallas_call | solution.py:414
  44.9 1.2 %finish.1 = (f32[2,32,1280]{2,1,0:T(8,128)}, f32[2,32,5120]{2,1,0:T(8,128)}) custom-call(f32[2,32,5120]{2,1,0:T(8,128)S(1)} %get-tuple-element.10.q_done, f32[2,32,1280]{2,1,0:T(8,128)S(1)} %get-tuple-element.11.p_done, f32[2,16,8,256]{3,2,1,0:T(8,128)S(1)} %get-tuple-element.12.refs_0_, f32[2,16,8,256]{3,2,1,0:T(8,128)S(1)} %get-tuple-element.13.refs_1_, ...), custom_call_target="tpu_custom_call" | custom-call | tf_op jit(solution)/shard_map/finish/pallas_call | solution.py:448

commit v9 on v8

--- a/solution.py
+++ b/solution.py
@@ -19,6 +19,7 @@
 STARTS = tuple(sum(WIDTHS[:k]) for k in range(len(WIDTHS)))
 P_STARTS = tuple(sum(P_WIDTHS[:k]) for k in range(len(P_WIDTHS)))
 Z_CHUNKS, P_CHUNKS = len(WIDTHS), len(P_WIDTHS)
+TURN = 1
 Z_HALF, P_HALF = sum(WIDTHS), sum(P_WIDTHS)
 
 
@@ -30,7 +31,6 @@
 CUBE = sorted([o for o in OFFSETS if hops(o) > 0], key=hops, reverse=True)
 PLANE = [o for o in CUBE if o[0] == 0]
 AXIS = [o for o in CUBE if o[1] == 0 and o[2] == 0]
-FLY = 5
 
 
 def dot(a, b, dims):
@@ -135,16 +135,30 @@
         row, column = jnp.where(core == 0, ys[d], y), jnp.where(core == 0, x, xs[d])
         return {"dp": (row * 4 + column) * 2 + core, "tensor": z}
 
+    def pick(zero, one):
+        return jnp.where(core == 0, zero, one)
+
+    def turns(l, k):
+        return (l + k) % 3, (l + k + TURN) % 3
+
+    def spun(turn, du, dv, dw):
+        dz, dy, dx = ((dw, du, dv), (dv, dw, du), (du, dv, dw))[turn]
+        return ys[dy], xs[dx], zs_at[dz]
+
     def spin(l, k, du, dv, dw):
-        return ((dw, du, dv), (dv, dw, du), (du, dv, dw))[(l + k) % 3]
-
-    def seat(l, k, offset):
-        dz, dy, dx = offset
-        u, v = ((ys[dy], xs[dx]), (xs[dx], zs_at[dz]), (zs_at[dz], ys[dy]))[(l + k) % 3]
-        return u * 4 + v
+        to_y, to_x, to_z = (pick(p, q) for p, q in zip(*(spun(t, du, dv, dw) for t in turns(l, k))))
+        return {"dp": (to_y * 4 + to_x) * 2 + core, "tensor": to_z}
+
+    def seat(l, k, du, dv):
+        seats = []
+        for t in turns(l, k):
+            to_y, to_x, to_z = spun(t, du, dv, 0)
+            u, v = ((to_y, to_x), (to_x, to_z), (to_z, to_y))[t]
+            seats.append(u * 4 + v)
+        return pick(*seats)
 
     def line_at(l, k):
-        return (z, y, x)[(l + k) % 3]
+        return pick(*((z, y, x)[t] for t in turns(l, k)))
 
     def remote(src, dst, send, recv, device):
         return pltpu.make_async_remote_copy(
@@ -154,8 +168,8 @@
     pending = []
 
     def drain():
-        for done in pending:
-            done()
+        while pending:
+            pending.pop(0)()
 
     def all_of(ref, count, send, recv):
         view = ref.at[pl.ds(0, count)]
@@ -255,7 +269,7 @@
         cols = pl.ds(pl.multiple_of(h * Z_HALF + STARTS[k], 128), WIDTHS[k])
         return sum3(dot(y3, c[l, :, cols], NN))
 
-    def z_scatter(l, y3):
+    def z_pair(l, y3):
         for k in range(Z_CHUNKS):
             to_pieces(zx[l][k], z_part(l, k, other, y3))
             cp = remote(zx[l][k], zxr[l][k], zx_sem.at[l, k], zxr_sem.at[l, k], sibling)
@@ -263,14 +277,16 @@
             pending.append(cp.wait_send)
         for k in range(Z_CHUNKS):
             to_pieces(zs[l][k], z_part(l, k, mine, y3))
+
+    def z_scatter(l):
+        for k in range(Z_CHUNKS):
             remote(zx[l][k], zxr[l][k], zx_sem.at[l, k], zxr_sem.at[l, k], sibling).wait_recv()
             zs[l][k][...] += zxr[l][k][...]
-            me = seat(l, k, (0, 0, 0))
+            me = seat(l, k, 0, 0)
             for _, du, dv in PLANE:
-                offset = spin(l, k, du, dv, 0)
                 remote(
-                    zs[l][k].at[seat(l, k, offset)], zrr[l][k].at[me],
-                    zsend_sem.at[l, k, 0], zrs_sem.at[l, k], device(*offset),
+                    zs[l][k].at[seat(l, k, du, dv)], zrr[l][k].at[me],
+                    zsend_sem.at[l, k, 0], zrs_sem.at[l, k], spin(l, k, du, dv, 0),
                 ).start()
             pending.append(all_of(zs[l][k], 15, zsend_sem.at[l, k, 0], zrs_sem.at[l, k]).wait_send)
             zrr[l][k][me] = zs[l][k][me]
@@ -283,7 +299,7 @@
             slot = zl[l][k].at[w]
             for dw, _, _ in AXIS:
                 remote(
-                    slot, slot, zsend_sem.at[l, k, 1], zline_sem.at[l, k], device(*spin(l, k, 0, 0, dw))
+                    slot, slot, zsend_sem.at[l, k, 1], zline_sem.at[l, k], spin(l, k, 0, 0, dw)
                 ).start()
             pending.append(all_of(zl[l][k], 3, zsend_sem.at[l, k, 1], zline_sem.at[l, k]).wait_send)
 
@@ -291,12 +307,12 @@
         for k in range(Z_CHUNKS):
             src = zl[l][k]
             all_of(src, 3, zsend_sem.at[l, k, 1], zline_sem.at[l, k]).wait_recv()
-            me = seat(l, k, (0, 0, 0))
+            me = seat(l, k, 0, 0)
             zag[l][k][mine, me] = src[0] + src[1] + src[2] + src[3]
             own = zag[l][k].at[mine, me]
             for _, du, dv in PLANE:
                 remote(
-                    own, own, zsend_sem.at[l, k, 2], zag_sem.at[l, k, me // 4], device(*spin(l, k, du, dv, 0))
+                    own, own, zsend_sem.at[l, k, 2], zag_sem.at[l, k, me // 4], spin(l, k, du, dv, 0)
                 ).start()
             pending.append(all_of(zag[l][k].at[mine], 15, zsend_sem.at[l, k, 2], zag_sem.at[l, k, 0]).wait_send)
 
@@ -304,7 +320,7 @@
         for k in range(Z_CHUNKS):
             whole = zag[l][k].at[mine]
             for d in (0, 1, 3, 2):
-                u = lax.rem(seat(l, k, (0, 0, 0)) // 4 + d, 4)
+                u = lax.rem(seat(l, k, 0, 0) // 4 + d, 4)
                 block = zag[l][k].at[mine, pl.ds(u * 4, 3 if d == 0 else 4)]
                 remote(block, block, zsend_sem.at[l, k, 3], zag_sem.at[l, k, u], sibling).wait_recv()
                 block = zag[l][k].at[mine, pl.ds(u * 4, 4)]
@@ -335,13 +351,15 @@
     p_second(1)
     pl.semaphore_wait(near_sem, len(AXIS))
     p_third(0)
-    y3, p_mine, p_other = y_pieces(0)
-    z_scatter(0, y3)
-    g_first = gram_of(p_mine) + gram_of(p_other)
+    y3, *p_early = y_pieces(0)
+    z_pair(0, y3)
     p_third(1)
-    y3, p_mine, p_other = y_pieces(1)
-    z_scatter(1, y3)
-    g_second = gram_of(p_mine) + gram_of(p_other)
+    z_scatter(0)
+    y3, *p_late = y_pieces(1)
+    z_pair(1, y3)
+    z_scatter(1)
+    g_first = gram_of(p_early[0]) + gram_of(p_early[1])
+    g_second = gram_of(p_late[0]) + gram_of(p_late[1])
     zero = jnp.zeros((32, 32), F32)
     gram[z] = jnp.concatenate([g_first, zero, g_second, zero], axis=1)
     for offset in AXIS:
@@ -349,6 +367,8 @@
     pending.append(all_of(gram, 3, gsend_sem.at[0], g_sem.at[0]).wait_send)
     z_line(0)
     z_line(1)
+    sent = list(pending)
+    pending.clear()
     z_gather(0)
     z_gather(1)
     for offset in AXIS:
@@ -367,6 +387,8 @@
             for k in range(P_CHUNKS):
                 start = h * P_HALF + P_STARTS[k]
                 p_done[l, :, start : start + P_WIDTHS[k]] = sum3(dot(inverse[l], split3(pf[l][k][h]), NN)) * root
+    for done in sent:
+        done()
     z_forward(0)
     q_half(0, mine)
     z_finish(0)

time: 46.2 us -> 45.7 us (0.989)
  no operation moved by 1% of the time
where the time goes in v9:
time: 45.7 us; the launch traced here: 45.6 us
  Pallas kernels  45 us (98%)
  between operations  0.64 us (1%)
    pallas_call x1, Pallas kernels, local(): pl.pallas_call(functools.partial(exchange_kernel, root=float(width) ** 0....  43.8 us
    pallas_call x1, Pallas kernels, local(): pl.pallas_call(finish_kernel, out_shape=(jax.ShapeDtypeStruct((2, 32, 2 *...  1.2 us

profile of v9, /device:TPU:1, one launch (start us, length us, event | category | flops | bytes accessed | tf_op | source)
XLA Modules:
  0.0 45.6 jit_solution(323431454483586435)
XLA Ops:
  0.6 43.8 %exchange.1 = (f32[2,32,5120]{2,1,0:T(8,128)S(1)}, f32[2,32,1280]{2,1,0:T(8,128)S(1)}, f32[2,16,8,256]{3,2,1,0:T(8,128)S(1)}, f32[2,16,8,256]{3,2,1,0:T(8,128)S(...) custom-call(bf16[2,512,1280]{2,1,0:T(8,128)(2,1)} %a_hbm.1, bf16[2,512,5120]{2,1,0:T(8,128)(2,1)} %c_hbm.1, ...), custom_call_target="tpu_custom_call" | custom-call | tf_op jit(solution)/shard_map/exchange/pallas_call | solution.py:436
  44.4 1.2 %finish.1 = (f32[2,32,1280]{2,1,0:T(8,128)}, f32[2,32,5120]{2,1,0:T(8,128)}) custom-call(f32[2,32,5120]{2,1,0:T(8,128)S(1)} %get-tuple-element.10.q_done, f32[2,32,1280]{2,1,0:T(8,128)S(1)} %get-tuple-element.11.p_done, f32[2,16,8,256]{3,2,1,0:T(8,128)S(1)} %get-tuple-element.12.refs_0_, f32[2,16,8,256]{3,2,1,0:T(8,128)S(1)} %get-tuple-element.13.refs_1_, ...), custom_call_target="tpu_custom_call" | custom-call | tf_op jit(solution)/shard_map/finish/pallas_call | solution.py:470

commit v10 on v9

--- a/solution.py
+++ b/solution.py
@@ -366,15 +366,17 @@
         remote(gram.at[z], gram.at[z], gsend_sem.at[0], g_sem.at[z], device(*offset)).start()
     pending.append(all_of(gram, 3, gsend_sem.at[0], g_sem.at[0]).wait_send)
     z_line(0)
+    for offset in AXIS:
+        _, from_z = back_from(*offset)
+        remote(gram.at[from_z], gram.at[from_z], gsend_sem.at[0], g_sem.at[from_z], sibling).wait_recv()
+    work = eliminate(gram[0] + gram[1] + gram[2] + gram[3], range(0), True)
     z_line(1)
     sent = list(pending)
     pending.clear()
     z_gather(0)
+    work = eliminate(work, range(0, 14))
     z_gather(1)
-    for offset in AXIS:
-        _, from_z = back_from(*offset)
-        remote(gram.at[from_z], gram.at[from_z], gsend_sem.at[0], g_sem.at[from_z], sibling).wait_recv()
-    inv_ref[...] = eliminate(gram[0] + gram[1] + gram[2] + gram[3], range(32), True)
+    inv_ref[...] = eliminate(work, range(14, 32))
     inverse = [factor(inv_ref, l) for l in range(2)]
 
     def q_half(l, h):

time: 45.7 us -> 45.5 us (level)
  no operation moved by 1% of the time
where the time goes in v10:
time: 45.5 us; the launch traced here: 45.4 us
  Pallas kernels  44.8 us (98%)
  between operations  0.64 us (1%)
    pallas_call x1, Pallas kernels, local(): pl.pallas_call(functools.partial(exchange_kernel, root=float(width) ** 0....  43.5 us
    pallas_call x1, Pallas kernels, local(): pl.pallas_call(finish_kernel, out_shape=(jax.ShapeDtypeStruct((2, 32, 2 *...  1.2 us

profile of v10, /device:TPU:1, one launch (start us, length us, event | category | flops | bytes accessed | tf_op | source)
XLA Modules:
  0.0 45.4 jit_solution(508647423074335282)
XLA Ops:
  0.6 43.5 %exchange.1 = (f32[2,32,5120]{2,1,0:T(8,128)S(1)}, f32[2,32,1280]{2,1,0:T(8,128)S(1)}, f32[2,16,8,256]{3,2,1,0:T(8,128)S(1)}, f32[2,16,8,256]{3,2,1,0:T(8,128)S(...) custom-call(bf16[2,512,1280]{2,1,0:T(8,128)(2,1)} %a_hbm.1, bf16[2,512,5120]{2,1,0:T(8,128)(2,1)} %c_hbm.1, ...), custom_call_target="tpu_custom_call" | custom-call | tf_op jit(solution)/shard_map/exchange/pallas_call | solution.py:438
  44.2 1.2 %finish.1 = (f32[2,32,1280]{2,1,0:T(8,128)}, f32[2,32,5120]{2,1,0:T(8,128)}) custom-call(f32[2,32,5120]{2,1,0:T(8,128)S(1)} %get-tuple-element.10.q_done, f32[2,32,1280]{2,1,0:T(8,128)S(1)} %get-tuple-element.11.p_done, f32[2,16,8,256]{3,2,1,0:T(8,128)S(1)} %get-tuple-element.12.refs_0_, f32[2,16,8,256]{3,2,1,0:T(8,128)S(1)} %get-tuple-element.13.refs_1_, ...), custom_call_target="tpu_custom_call" | custom-call | tf_op jit(solution)/shard_map/finish/pallas_call | solution.py:472

commit v11 on v10

--- a/solution.py
+++ b/solution.py
@@ -43,6 +43,10 @@
     mid = rest.astype(BF16)
     low = (rest - mid.astype(F32)).astype(BF16)
     return jnp.concatenate([hi, mid, low], axis=0)
+
+
+def sum2(x):
+    return x[0:32] + x[32:64]
 
 
 def sum3(x):
@@ -257,17 +261,17 @@
 
     def y_pieces(l):
         p_mine = half_pieces(l, mine)
-        y = sum3(dot(p_mine, a[l, :, half_of(mine)], NT))
+        y = sum2(dot(p_mine[0:64], a[l, :, half_of(mine)], NT))
         for k in range(P_CHUNKS):
             slot = pf[l][k].at[other]
             remote(slot, slot, psend_sem.at[l, k, 2], pfw_sem.at[l, k], sibling).wait_recv()
         p_other = half_pieces(l, other)
-        y = y + sum3(dot(p_other, a[l, :, half_of(other)], NT))
-        return split3(y * (1.0 / 32.0)), p_mine, p_other
+        y = y + sum2(dot(p_other[0:64], a[l, :, half_of(other)], NT))
+        return split3(y * (1.0 / 32.0))[0:64], p_mine, p_other
 
     def z_part(l, k, h, y3):
         cols = pl.ds(pl.multiple_of(h * Z_HALF + STARTS[k], 128), WIDTHS[k])
-        return sum3(dot(y3, c[l, :, cols], NN))
+        return sum2(dot(y3, c[l, :, cols], NN))
 
     def z_pair(l, y3):
         for k in range(Z_CHUNKS):

time: 45.5 us -> 45.5 us (level)
  no operation moved by 1% of the time
where the time goes in v11:
time: 45.5 us; the launch traced here: 45.4 us
  Pallas kernels  44.7 us (98%)
  between operations  0.64 us (1%)
    pallas_call x1, Pallas kernels, local(): pl.pallas_call(functools.partial(exchange_kernel, root=float(width) ** 0....  43.5 us
    pallas_call x1, Pallas kernels, local(): pl.pallas_call(finish_kernel, out_shape=(jax.ShapeDtypeStruct((2, 32, 2 *...  1.2 us

profile of v11, /device:TPU:1, one launch (start us, length us, event | category | flops | bytes accessed | tf_op | source)
XLA Modules:
  0.0 45.4 jit_solution(2981023341362330379)
XLA Ops:
  0.6 43.5 %exchange.1 = (f32[2,32,5120]{2,1,0:T(8,128)S(1)}, f32[2,32,1280]{2,1,0:T(8,128)S(1)}, f32[2,16,8,256]{3,2,1,0:T(8,128)S(1)}, f32[2,16,8,256]{3,2,1,0:T(8,128)S(...) custom-call(bf16[2,512,1280]{2,1,0:T(8,128)(2,1)} %a_hbm.1, bf16[2,512,5120]{2,1,0:T(8,128)(2,1)} %c_hbm.1, ...), custom_call_target="tpu_custom_call" | custom-call | tf_op jit(solution)/shard_map/exchange/pallas_call | solution.py:442
  44.2 1.2 %finish.1 = (f32[2,32,1280]{2,1,0:T(8,128)}, f32[2,32,5120]{2,1,0:T(8,128)}) custom-call(f32[2,32,5120]{2,1,0:T(8,128)S(1)} %get-tuple-element.10.q_done, f32[2,32,1280]{2,1,0:T(8,128)S(1)} %get-tuple-element.11.p_done, f32[2,16,8,256]{3,2,1,0:T(8,128)S(1)} %get-tuple-element.12.refs_0_, f32[2,16,8,256]{3,2,1,0:T(8,128)S(1)} %get-tuple-element.13.refs_1_, ...), custom_call_target="tpu_custom_call" | custom-call | tf_op jit(solution)/shard_map/finish/pallas_call | solution.py:476

commit v12 on v10

--- a/solution.py
+++ b/solution.py
@@ -374,9 +374,9 @@
     sent = list(pending)
     pending.clear()
     z_gather(0)
-    work = eliminate(work, range(0, 14))
+    work = eliminate(work, range(0, 18))
     z_gather(1)
-    inv_ref[...] = eliminate(work, range(14, 32))
+    inv_ref[...] = eliminate(work, range(18, 32))
     inverse = [factor(inv_ref, l) for l in range(2)]
 
     def q_half(l, h):

time: 45.5 us -> 45.5 us (level)
  no operation moved by 1% of the time
where the time goes in v12:
time: 45.5 us; the launch traced here: 45.4 us
  Pallas kernels  44.8 us (98%)
  between operations  0.64 us (1%)
    pallas_call x1, Pallas kernels, local(): pl.pallas_call(functools.partial(exchange_kernel, root=float(width) ** 0....  43.5 us
    pallas_call x1, Pallas kernels, local(): pl.pallas_call(finish_kernel, out_shape=(jax.ShapeDtypeStruct((2, 32, 2 *...  1.2 us

profile of v12, /device:TPU:1, one launch (start us, length us, event | category | flops | bytes accessed | tf_op | source)
XLA Modules:
  0.0 45.4 jit_solution(1494186505763149099)
XLA Ops:
  0.6 43.5 %exchange.1 = (f32[2,32,5120]{2,1,0:T(8,128)S(1)}, f32[2,32,1280]{2,1,0:T(8,128)S(1)}, f32[2,16,8,256]{3,2,1,0:T(8,128)S(1)}, f32[2,16,8,256]{3,2,1,0:T(8,128)S(...) custom-call(bf16[2,512,1280]{2,1,0:T(8,128)(2,1)} %a_hbm.1, bf16[2,512,5120]{2,1,0:T(8,128)(2,1)} %c_hbm.1, ...), custom_call_target="tpu_custom_call" | custom-call | tf_op jit(solution)/shard_map/exchange/pallas_call | solution.py:438
  44.2 1.2 %finish.1 = (f32[2,32,1280]{2,1,0:T(8,128)}, f32[2,32,5120]{2,1,0:T(8,128)}) custom-call(f32[2,32,5120]{2,1,0:T(8,128)S(1)} %get-tuple-element.10.q_done, f32[2,32,1280]{2,1,0:T(8,128)S(1)} %get-tuple-element.11.p_done, f32[2,16,8,256]{3,2,1,0:T(8,128)S(1)} %get-tuple-element.12.refs_0_, f32[2,16,8,256]{3,2,1,0:T(8,128)S(1)} %get-tuple-element.13.refs_1_, ...), custom_call_target="tpu_custom_call" | custom-call | tf_op jit(solution)/shard_map/finish/pallas_call | solution.py:472
